TPU v7x, 32 devices: a whole 2x2x4 slice. The times are simulated.
32 devices in a mesh: vol: 16 (over z, y, x), src: 2 (over core).
Axes of the slice: x: 2, y: 2, z: 4, core: 2. Of those that a mesh axis runs over, the one named last changes fastest.
Arguments:
- excitation: float32 [32, 32, 32, 128], P(None, 'vol', 'src'), may hold values from -6 to 6
- start: float32 [32, 32, 32, 128], P(None, 'vol', 'src'), may hold values from -4 to 4
- material: int32 [32, 32, 128], P('vol', 'src'), may hold values from 0 to 2
- face_cell: int32 [16, 2, 64], P('vol', 'src'), may hold values from 0 to 4095
- face_count: int32 [16, 2, 16], P('vol', 'src'), may hold values from 0 to 4, as said below
- face_weight: float32 [16, 2, 64], P('vol', 'src'), may hold values from 0.5 to 1.5
- slot_panel: int32 [16, 2, 64], P('vol', 'src'), may hold values from 0 to 2047
- target_points: float32 [3, 65536], P(None, 'vol'), may hold values from 0 to 1
- source_points: float32 [3, 65536], P(None, 'src'), may hold values from 0 to 1
Outputs:
- potential: float32 [32, 32, 32, 128], P(None, 'vol', 'src')
- flux: float32 [32, 65536], P(None, ('vol', 'src'))
Inputs may be any that keep to these rules, and one draw needn't show every extreme that they name: A device has at most 4 live slots for one owner (the first face_count ones); in every draw some owner receives 4 live faces from every device.
All inputs are finite; a program needn't handle non-finite values.
Results may differ from a plain program's by a relative error of at most 0.0023.
The roundings to bfloat16 on the way count: a program that leaves them out, or rounds other values in their place, can miss the bound.
Values may be sent and summed in bfloat16 or wider, within the bound.
A program may use at most 64 MiB of HBM per device.

v0:
```python
import jax
import jax.numpy as jnp
from jax import lax
from jax.sharding import PartitionSpec as P

P_SIZE = 65536
ITERS = 2
SWEEPS = 2


NU_BASE = (1.0, 0.05, 0.4)
NU_SATURATION = (0.0, 0.9, 0.3)
RELAXATION = 0.8
SOFTENING = 0.05


def extended(block, sides, width):
    for axis, dim in sides:
        count = lax.axis_size(axis)
        forward = [(i, i + 1) for i in range(count - 1)]
        backward = [(target, source) for source, target in forward]
        low = lax.ppermute(
            lax.slice_in_dim(block, block.shape[dim] - width, None, axis=dim), axis, forward
        )
        high = lax.ppermute(lax.slice_in_dim(block, 0, width, axis=dim), axis, backward)
        block = jnp.concatenate([low, block, high], axis=dim)
    return block


def reluctivity(grad_sq, material):
    base_value = jnp.zeros(material.shape, jnp.float32)
    slope_value = jnp.zeros(material.shape, jnp.float32)
    for material_id in range(3):
        picked = material == material_id
        base_value = jnp.where(picked, NU_BASE[material_id], base_value)
        slope_value = jnp.where(picked, NU_SATURATION[material_id], slope_value)
    return base_value[None] + slope_value[None] * grad_sq / (1.0 + grad_sq)


def gradient_sq(padded):
    along_x = 0.5 * (padded[:, 2:, 1:-1, 1:-1] - padded[:, :-2, 1:-1, 1:-1])
    along_y = 0.5 * (padded[:, 1:-1, 2:, 1:-1] - padded[:, 1:-1, :-2, 1:-1])
    along_z = 0.5 * (padded[:, 1:-1, 1:-1, 2:] - padded[:, 1:-1, 1:-1, :-2])
    return along_x * along_x + along_y * along_y + along_z * along_z


def pad_depth(values):
    return jnp.pad(values, ((0, 0), (0, 0), (0, 0), (1, 1)))


def face_weights(nu_ext, domain_edges):
    first_x, last_x, first_y, last_y = domain_edges
    interior = nu_ext[:, 1:-1, 1:-1]
    low_x = jnp.where(first_x, interior[:, :1], nu_ext[:, :1, 1:-1])
    high_x = jnp.where(last_x, interior[:, -1:], nu_ext[:, -1:, 1:-1])
    column = jnp.concatenate([low_x, interior, high_x], axis=1)
    low_y = jnp.where(first_y, interior[:, :, :1], nu_ext[:, 1:-1, :1])
    high_y = jnp.where(last_y, interior[:, :, -1:], nu_ext[:, 1:-1, -1:])
    row_ext = jnp.concatenate([low_y, interior, high_y], axis=2)
    depth_ext = jnp.pad(interior, ((0, 0), (0, 0), (0, 0), (1, 1)), mode="edge")
    return (
        0.5 * (interior + column[:, 2:]),
        0.5 * (interior + column[:, :-2]),
        0.5 * (interior + row_ext[:, :, 2:]),
        0.5 * (interior + row_ext[:, :, :-2]),
        0.5 * (interior + depth_ext[:, :, :, 2:]),
        0.5 * (interior + depth_ext[:, :, :, :-2]),
    )


def relax(padded, weights, diagonal, forcing):
    center = padded[:, 1:-1, 1:-1, 1:-1]
    neighbours = (
        padded[:, 2:, 1:-1, 1:-1],
        padded[:, :-2, 1:-1, 1:-1],
        padded[:, 1:-1, 2:, 1:-1],
        padded[:, 1:-1, :-2, 1:-1],
        padded[:, 1:-1, 1:-1, 2:],
        padded[:, 1:-1, 1:-1, :-2],
    )
    applied = diagonal * center
    for weight, neighbour in zip(weights, neighbours):
        applied = applied - weight * neighbour
    return center + RELAXATION * (forcing - applied) / diagonal


def with_rim(potential):
    return extended(potential, (("vol", 1), ("src", 2)), 1)


def per_device(
    excitation,
    start,
    material,
    face_cell,
    face_count,
    face_weight,
    slot_panel,
    target_points,
    source_points,
):
    vol_count = lax.axis_size("vol")
    first_x = lax.axis_index("vol") == 0
    last_x = lax.axis_index("vol") == vol_count - 1
    first_y = lax.axis_index("src") == 0
    last_y = lax.axis_index("src") == lax.axis_size("src") - 1
    domain_edges = (first_x, last_x, first_y, last_y)
    exc_count, width_x, width_y, depth_len = excitation.shape
    cell_count = width_x * width_y * depth_len
    slot_cells = face_cell.reshape(-1)
    slot_count = slot_cells.shape[0]
    capacity = slot_count // vol_count
    piece_len = source_points.shape[1] // vol_count
    target_len = target_points.shape[1]
    slot_rank = jnp.arange(slot_count, dtype=jnp.int32) % capacity
    live_count = jnp.repeat(face_count.reshape(-1), capacity, total_repeat_length=slot_count)
    slot_scale = jnp.where(slot_rank < live_count, face_weight.reshape(-1), 0.0)
    owner_table = (
        slot_panel.reshape(-1)[:, None] == jnp.arange(piece_len, dtype=jnp.int32)[None, :]
    ).astype(jnp.float32)
    flux_scale = float(P_SIZE) ** (-0.5)
    potential = start
    flux_own = jnp.zeros((exc_count, piece_len), jnp.float32)
    for outer_index in range(ITERS):
        current = with_rim(potential)
        nu_own = reluctivity(gradient_sq(pad_depth(current)), material)
        nu_ext = extended(nu_own, (("vol", 1), ("src", 2)), 1)
        weights = face_weights(nu_ext, domain_edges)
        diagonal = weights[0] + weights[1] + weights[2] + weights[3] + weights[4] + weights[5]
        cell_values = jnp.take(potential.reshape(exc_count, cell_count), slot_cells, axis=1)
        outgoing = (cell_values * slot_scale[None, :]).T.reshape(vol_count, capacity * exc_count)
        arrived = lax.all_to_all(outgoing, "vol", split_axis=0, concat_axis=0, tiled=True).reshape(
            slot_count, exc_count
        )
        density = jnp.dot(
            arrived.T,
            owner_table,
            precision=lax.Precision.HIGHEST,
            preferred_element_type=jnp.float32,
        ).astype(jnp.bfloat16)
        block_piece = lax.all_gather(density, "vol", axis=1, tiled=True)
        piece_count = block_piece.shape[1]
        step_len = 1024

        def one_step(step_index, partial_value):
            offset_index = step_index * step_len
            segment = lax.dynamic_slice_in_dim(block_piece, offset_index, step_len, 1)
            places = lax.dynamic_slice_in_dim(source_points, offset_index, step_len, 1)
            dist_sq = jnp.zeros((target_len, step_len), jnp.float32)
            for component in range(3):
                offset = target_points[component][:, None] - places[component][None, :]
                dist_sq = dist_sq + offset * offset
            kernel = lax.rsqrt(dist_sq + SOFTENING * SOFTENING).astype(jnp.bfloat16)
            return partial_value + jnp.einsum(
                "en,tn->et", segment, kernel, preferred_element_type=jnp.float32
            )

        partial_flux = lax.fori_loop(
            0, piece_count // step_len, one_step, jnp.zeros((exc_count, target_len), jnp.float32)
        )
        flux_sum = lax.psum_scatter(partial_flux, "src", scatter_dimension=1, tiled=True)
        flux_own = flux_sum * flux_scale
        per_slot = jnp.dot(
            flux_own,
            owner_table.T,
            precision=lax.Precision.HIGHEST,
            preferred_element_type=jnp.float32,
        )
        returned = lax.all_to_all(
            per_slot.T.reshape(vol_count, capacity * exc_count),
            "vol",
            split_axis=0,
            concat_axis=0,
            tiled=True,
        ).reshape(slot_count, exc_count)
        contribution = returned.T * slot_scale[None, :]
        surface = (
            jnp.zeros((exc_count, cell_count), jnp.float32).at[:, slot_cells].add(contribution)
        )
        forcing = excitation + surface.reshape(excitation.shape)
        for sweep_index in range(SWEEPS):
            if sweep_index > 0:
                current = with_rim(potential)
            potential = relax(pad_depth(current), weights, diagonal, forcing)
    return (potential, flux_own)


def solution(mesh):
    return jax.shard_map(
        per_device,
        mesh=mesh,
        in_specs=(
            P(None, "vol", "src", None),
            P(None, "vol", "src", None),
            P("vol", "src", None),
            P("vol", "src", None),
            P("vol", "src", None),
            P("vol", "src", None),
            P("vol", "src", None),
            P(None, "vol"),
            P(None, "src"),
        ),
        out_specs=(P(None, "vol", "src", None), P(None, ("vol", "src"))),
        check_vma=False,
    )
```

profile of v0, /device:TPU:0, one launch (start us, length us, event | category | flops | bytes accessed | tf_op | source)
XLA Modules:
  0.0 842.4 jit_solution(2752922507507373458)
XLA Ops:
  12.6 15.4 %all_to_all.36 = f32[16,1,128]{2,1,0:T(1,128)S(1)} all-to-all(f32[16,1,128]{2,1,0:T(1,128)S(1)} %bitcast.88), channel_id=1, replica_groups=mesh['vol'=16,'src'=2] {'vol'}, dimensions={0} | all-to-all | bytes 16384 | tf_op jit(solution)/shard_map/all_to_all | solution.py:132
  34.3 8.9 %collective-permute-done.1 = f32[32,1,16,128]{3,2,1,0:T(8,128)S(1)} collective-permute-done((f32[32,1,16,128]{3,2,1,0:T(8,128)S(1)}, f32[32,1,16,128]{3,2,1,0:T(8,128)S(1)}, u32[]{:S(2)}, u32[]{:S(2)}) %collective-permute-start.1) | collective-permute-done | bytes 262176 | tf_op jit(solution)/shard_map/ppermute | solution.py:22
  53.2 36.8 %all-gather.3.cloned.1.call-done = bf16[32,32768]{1,0:T(8,128)(2,1)} async-done(((bf16[32,2048]{1,0:T(8,128)(2,1)}), bf16[32,32768]{1,0:T(8,128)(2,1)}) %all-gather.3.cloned.1.call-update) | async-done | bytes 2097168 | tf_op jit(solution)/shard_map/all_gather | solution.py:141
  90.1 263.1 %while.29 = (s32[]{:T(128)}, f32[32,4096]{1,0:T(8,128)S(1)}, bf16[32,32768]{1,0:T(8,128)(2,1)}, f32[3,4096]{1,0:T(4,128)S(1)}, f32[3,32768]{1,0:T(4,128)}, /*ind...) while((s32[]{:T(128)}, f32[32,4096]{1,0:T(8,128)S(1)}, ...), condition=%wide.region_1.3_spmd.clone, body=%wide.region_0.2_spmd.clone.sunk | while | flops 310640640 | bytes 1298645 | solution.py:158
  91.0 7.3 fusion.105
  107.5 7.3 fusion.105
  123.9 7.3 fusion.105
  132.1 7.3 fusion.105
  148.6 7.3 fusion.105
  156.8 7.3 fusion.105
  173.2 7.3 fusion.105
  181.5 7.3 fusion.105
  197.9 7.3 fusion.105
  206.1 7.3 fusion.105
  222.6 7.3 fusion.105
  230.8 7.3 fusion.105
  247.2 7.3 fusion.105
  255.5 7.3 fusion.105
  271.9 7.3 fusion.105
  280.1 7.3 fusion.105
  296.6 7.3 fusion.105
  304.8 7.3 fusion.105
  321.2 7.3 fusion.105
  329.5 7.3 fusion.105
  345.9 7.3 fusion.105
  363.6 8.3 collective-permute-done.4
  407.9 10.3 %collective-permute-done.9 = f32[32,1,16,128]{3,2,1,0:T(8,128)S(1)} collective-permute-done((f32[32,1,16,128]{3,2,1,0:T(8,128)S(1)}, f32[32,1,16,128]{3,2,1,0:T(8,128)S(1)}, u32[]{:S(2)}, u32[]{:S(2)}) %collective-permute-start.9) | collective-permute-done | bytes 262176 | tf_op jit(solution)/shard_map/ppermute | solution.py:22
  429.8 11.4 %all_to_all.37 = f32[16,1,128]{2,1,0:T(1,128)S(1)} all-to-all(f32[16,1,128]{2,1,0:T(1,128)S(1)} %bitcast.89), channel_id=1, replica_groups=mesh['vol'=16,'src'=2] {'vol'}, dimensions={0} | all-to-all | bytes 16384 | tf_op jit(solution)/shard_map/all_to_all | solution.py:132
  447.0 9.2 %collective-permute-done.13 = f32[32,1,16,128]{3,2,1,0:T(8,128)S(1)} collective-permute-done((f32[32,1,16,128]{3,2,1,0:T(8,128)S(1)}, f32[32,1,16,128]{3,2,1,0:T(8,128)S(1)}, u32[]{:S(2)}, u32[]{:S(2)}) %collective-permute-start.13) | collective-permute-done | bytes 262176 | tf_op jit(solution)/shard_map/ppermute | solution.py:22
  466.5 36.5 %all-gather.5.cloned.1.call-done = bf16[32,32768]{1,0:T(8,128)(2,1)} async-done(((bf16[32,2048]{1,0:T(8,128)(2,1)}), bf16[32,32768]{1,0:T(8,128)(2,1)}) %all-gather.5.cloned.1.call-update) | async-done | bytes 2097168 | tf_op jit(solution)/shard_map/all_gather | solution.py:141
  502.9 263.0 %while.30 = (s32[]{:T(128)}, f32[32,4096]{1,0:T(8,128)S(1)}, bf16[32,32768]{1,0:T(8,128)(2,1)}, f32[3,4096]{1,0:T(4,128)S(1)}, f32[3,32768]{1,0:T(4,128)}, /*ind...) while((s32[]{:T(128)}, f32[32,4096]{1,0:T(8,128)S(1)}, ...), condition=%wide.region_5.7_spmd.clone, body=%wide.region_4.6_spmd.clone.sunk | while | flops 310640640 | bytes 1298645 | solution.py:158
  512.1 7.3 fusion.108
  528.5 7.3 fusion.108
  536.7 7.3 fusion.108
  545.0 7.3 fusion.108
  553.2 7.3 fusion.108
  586.1 7.3 fusion.108
  594.3 7.3 fusion.108
  627.2 7.3 fusion.108
  643.6 7.3 fusion.108
  651.8 7.3 fusion.108
  660.0 7.3 fusion.108
  668.3 7.3 fusion.108
  701.1 7.3 fusion.108
  709.4 7.3 fusion.108
  758.7 7.3 fusion.108
  776.4 8.3 collective-permute-done.16
  815.5 9.7 %collective-permute-done.21 = f32[32,1,16,128]{3,2,1,0:T(8,128)S(1)} collective-permute-done((f32[32,1,16,128]{3,2,1,0:T(8,128)S(1)}, f32[32,1,16,128]{3,2,1,0:T(8,128)S(1)}, u32[]{:S(2)}, u32[]{:S(2)}) %collective-permute-start.21) | collective-permute-done | bytes 262176 | tf_op jit(solution)/shard_map/ppermute | solution.py:22
  (346 shorter events, 411.2 us)
Async XLA Ops:
  7.2 23.2 %copy-start.1 = (f32[32,2,16,128]{3,2,1,0:T(8,128)S(1)}, f32[32,2,16,128]{3,2,1,0:T(8,128)}, u32[]{:S(2)}) copy-start(f32[32,2,16,128]{3,2,1,0:T(8,128)} %param.18) | copy-start | bytes 1572868
  7.2 27.1 %copy-start.25 = (s32[2,16,128]{2,1,0:T(8,128)S(1)}, s32[2,16,128]{2,1,0:T(8,128)}, u32[]{:S(2)}) copy-start(s32[2,16,128]{2,1,0:T(8,128)} %param.19) | copy-start | bytes 49156
  7.2 82.8 %all-gather.3.cloned.1.call-start = ((), (), s32[]{:S(2)}) async-start(), calls=%async_computation.6 | async-start | bytes 2228224 | tf_op jit(solution)/shard_map/all_gather | solution.py:141
  8.0 35.3 %copy-start.29 = (pred[64]{0:T(512)(128)(4,1)}, pred[64]{0:T(512)(128)(4,1)S(1)}, u32[]{:S(2)}) copy-start(pred[64]{0:T(512)(128)(4,1)S(1)} %compare_and_fusion) | copy-start | bytes 196
  8.7 39.6 %copy-start.32 = (s32[1,1,64]{2,1,0:T(1,128)S(1)}, s32[1,1,64]{2,1,0:T(1,128)}, u32[]{:S(2)}) copy-start(s32[1,1,64]{2,1,0:T(1,128)} %param.20) | copy-start | bytes 772
  11.0 42.2 %copy-start.26 = (s32[1024]{0:T(1024)}, s32[1024]{0:T(1024)S(1)}, u32[]{:S(2)}) copy-start(s32[1024]{0:T(1024)S(1)} %get-tuple-element.316) | copy-start | bytes 12292
  30.4 346.3 %reduce-scatter.3.cloned.1.call-start = ((), (), s32[]{:S(2)}) async-start(), calls=%async_computation.7 | async-start | bytes 786432 | tf_op jit(solution)/shard_map/reduce_scatter | solution.py:161
  30.5 12.7 %collective-permute-start.1 = (f32[32,1,16,128]{3,2,1,0:T(8,128)S(1)}, f32[32,1,16,128]{3,2,1,0:T(8,128)S(1)}, u32[]{:S(2)}, u32[]{:S(2)}) collective-permute-start(f32[32,1,16,128]{3,2,1,0:T(8,128)S(1)} %get-tuple-element.312), channel_id=1, source_target_pairs={{0,2},{2,4},{4,6},{6,8},{8,10},{10,12},{12,14},{14,16},{16,18},{18... | collective-permute-start | bytes 786440 | tf_op jit(solution)/shard_map/ppermute | solution.py:22
  33.0 12.6 %collective-permute-start = (f32[32,1,16,128]{3,2,1,0:T(8,128)S(1)}, f32[32,1,16,128]{3,2,1,0:T(8,128)S(1)}, u32[]{:S(2)}, u32[]{:S(2)}) collective-permute-start(f32[32,1,16,128]{3,2,1,0:T(8,128)S(1)} %get-tuple-element.311), channel_id=1, source_target_pairs={{2,0},{4,2},{6,4},{8,6},{10,8},{12,10},{14,12},{16,14},{18,16},{20... | collective-permute-start | bytes 786440 | tf_op jit(solution)/shard_map/ppermute | solution.py:25
  34.3 319.7 %copy-start.21 = (f32[2,16,128]{2,1,0:T(8,128)}, f32[2,16,128]{2,1,0:T(8,128)S(1)}, u32[]{:S(2)}) copy-start(f32[2,16,128]{2,1,0:T(8,128)S(1)} %get-tuple-element.313) | copy-start | bytes 49156
  34.3 319.7 %copy-start.23 = (f32[2,16,128]{2,1,0:T(8,128)}, f32[2,16,128]{2,1,0:T(8,128)S(1)}, u32[]{:S(2)}) copy-start(f32[2,16,128]{2,1,0:T(8,128)S(1)} %get-tuple-element.314) | copy-start | bytes 49156
  43.2 46.8 %copy-start.5 = (f32[3,4096]{1,0:T(4,128)S(1)}, f32[3,4096]{1,0:T(4,128)}, u32[]{:S(2)}) copy-start(f32[3,4096]{1,0:T(4,128)} %param.24) | copy-start | bytes 147460
  45.6 308.4 %copy-start.6 = (f32[32,1,16,128]{3,2,1,0:T(8,128)}, f32[32,1,16,128]{3,2,1,0:T(8,128)S(1)}, u32[]{:S(2)}) copy-start(f32[32,1,16,128]{3,2,1,0:T(8,128)S(1)} %collective-permute-done) | copy-start | bytes 786436
  45.7 3.2 collective-permute-start.3
  47.0 3.1 collective-permute-start.2
  50.2 303.9 %copy-start.14 = (f32[32,4,1,128]{3,2,1,0:T(1,128)}, f32[32,4,1,128]{3,2,1,0:T(1,128)S(1)}, u32[]{:S(2)}) copy-start(f32[32,4,1,128]{3,2,1,0:T(1,128)S(1)} %collective-permute-done.2) | copy-start | bytes 196612
  356.3 7.3 collective-permute-start.5
  359.0 12.9 %collective-permute-start.4 = (f32[32,1,16,128]{3,2,1,0:T(8,128)S(1)}, f32[32,1,16,128]{3,2,1,0:T(8,128)S(1)}, u32[]{:S(2)}, u32[]{:S(2)}) collective-permute-start(f32[32,1,16,128]{3,2,1,0:T(8,128)S(1)} %get-tuple-element.310), channel_id=1, source_target_pairs={{2,0},{4,2},{6,4},{8,6},{10,8},{12,10},{14,12},{16,14},{18,16},{20... | collective-permute-start | bytes 786440 | tf_op jit(solution)/shard_map/ppermute | solution.py:25
  372.6 12.9 %collective-permute-start.7 = (f32[32,4,1,128]{3,2,1,0:T(1,128)}, f32[32,4,1,128]{3,2,1,0:T(1,128)}, u32[]{:S(2)}, u32[]{:S(2)}) collective-permute-start(f32[32,4,1,128]{3,2,1,0:T(1,128)} %get-tuple-element.285), channel_id=1, source_target_pairs={{0,1},{2,3},{4,5},{6,7},{8,9},{10,11},{12,13},{14,15},{16,17},{18,... | collective-permute-start | bytes 196616 | tf_op jit(solution)/shard_map/ppermute | solution.py:22
  374.5 11.0 %collective-permute-start.6 = (f32[32,4,1,128]{3,2,1,0:T(1,128)}, f32[32,4,1,128]{3,2,1,0:T(1,128)}, u32[]{:S(2)}, u32[]{:S(2)}) collective-permute-start(f32[32,4,1,128]{3,2,1,0:T(1,128)} %get-tuple-element.286), channel_id=1, source_target_pairs={{1,0},{3,2},{5,4},{7,6},{9,8},{11,10},{13,12},{15,14},{17,16},{19,... | collective-permute-start | bytes 196616 | tf_op jit(solution)/shard_map/ppermute | solution.py:25
  380.1 12.5 %all-to-all-start.1 = ((f32[16,1,128]{2,1,0:T(1,128)}), f32[16,1,128]{2,1,0:T(1,128)}, u32[]{:S(2)}, u32[]{:S(2)}) async-start(f32[16,1,128]{2,1,0:T(1,128)} %bitcast.10), calls=%async_computation.2 | async-start | bytes 16384 | tf_op jit(solution)/shard_map/all_to_all | solution.py:169
  385.5 117.5 %all-gather.5.cloned.1.call-start = ((), (), s32[]{:S(2)}) async-start(), calls=%async_computation.8 | async-start | bytes 2228224 | tf_op jit(solution)/shard_map/all_gather | solution.py:141
  403.7 23.2 %copy-start.9 = (f32[32,1,16,128]{3,2,1,0:T(8,128)S(1)}, f32[32,1,16,128]{3,2,1,0:T(8,128)}, u32[]{:S(2)}) copy-start(f32[32,1,16,128]{3,2,1,0:T(8,128)} %get-tuple-element.305) | copy-start | bytes 786436
  403.7 23.2 %copy-start.10 = (f32[32,1,16,128]{3,2,1,0:T(8,128)S(1)}, f32[32,1,16,128]{3,2,1,0:T(8,128)}, u32[]{:S(2)}) copy-start(f32[32,1,16,128]{3,2,1,0:T(8,128)} %get-tuple-element.306) | copy-start | bytes 786436
  403.8 23.2 %copy-start.19 = (f32[32,2,1,128]{3,2,1,0:T(1,128)S(1)}, f32[32,2,1,128]{3,2,1,0:T(1,128)}, u32[]{:S(2)}) copy-start(f32[32,2,1,128]{3,2,1,0:T(1,128)} %get-tuple-element.307) | copy-start | bytes 98308
  403.8 23.2 %copy-start.20 = (f32[32,2,1,128]{3,2,1,0:T(1,128)S(1)}, f32[32,2,1,128]{3,2,1,0:T(1,128)}, u32[]{:S(2)}) copy-start(f32[32,2,1,128]{3,2,1,0:T(1,128)} %get-tuple-element.308) | copy-start | bytes 98308
  403.8 14.4 %collective-permute-start.9 = (f32[32,1,16,128]{3,2,1,0:T(8,128)S(1)}, f32[32,1,16,128]{3,2,1,0:T(8,128)S(1)}, u32[]{:S(2)}, u32[]{:S(2)}) collective-permute-start(f32[32,1,16,128]{3,2,1,0:T(8,128)S(1)} %get-tuple-element.301), channel_id=1, source_target_pairs={{0,2},{2,4},{4,6},{6,8},{8,10},{10,12},{12,14},{14,16},{16,18},{18... | collective-permute-start | bytes 786440 | tf_op jit(solution)/shard_map/ppermute | solution.py:22
  406.6 13.5 %collective-permute-start.8 = (f32[32,1,16,128]{3,2,1,0:T(8,128)S(1)}, f32[32,1,16,128]{3,2,1,0:T(8,128)S(1)}, u32[]{:S(2)}, u32[]{:S(2)}) collective-permute-start(f32[32,1,16,128]{3,2,1,0:T(8,128)S(1)} %get-tuple-element.302), channel_id=1, source_target_pairs={{2,0},{4,2},{6,4},{8,6},{10,8},{12,10},{14,12},{16,14},{18,16},{20... | collective-permute-start | bytes 786440 | tf_op jit(solution)/shard_map/ppermute | solution.py:25
  420.2 2.9 collective-permute-start.11
  421.6 3.1 collective-permute-start.10
  443.0 345.2 %reduce-scatter.5.cloned.1.call-start = ((), (), s32[]{:S(2)}) async-start(), calls=%async_computation.9 | async-start | bytes 786432 | tf_op jit(solution)/shard_map/reduce_scatter | solution.py:161
  443.1 13.0 %collective-permute-start.13 = (f32[32,1,16,128]{3,2,1,0:T(8,128)S(1)}, f32[32,1,16,128]{3,2,1,0:T(8,128)S(1)}, u32[]{:S(2)}, u32[]{:S(2)}) collective-permute-start(f32[32,1,16,128]{3,2,1,0:T(8,128)S(1)} %get-tuple-element.299), channel_id=1, source_target_pairs={{0,2},{2,4},{4,6},{6,8},{8,10},{10,12},{12,14},{14,16},{16,18},{18... | collective-permute-start | bytes 786440 | tf_op jit(solution)/shard_map/ppermute | solution.py:22
  445.7 12.9 %collective-permute-start.12 = (f32[32,1,16,128]{3,2,1,0:T(8,128)S(1)}, f32[32,1,16,128]{3,2,1,0:T(8,128)S(1)}, u32[]{:S(2)}, u32[]{:S(2)}) collective-permute-start(f32[32,1,16,128]{3,2,1,0:T(8,128)S(1)} %get-tuple-element.300), channel_id=1, source_target_pairs={{2,0},{4,2},{6,4},{8,6},{10,8},{12,10},{14,12},{16,14},{18,16},{20... | collective-permute-start | bytes 786440 | tf_op jit(solution)/shard_map/ppermute | solution.py:25
  458.6 308.2 %copy-start.4 = (f32[32,1,16,128]{3,2,1,0:T(8,128)}, f32[32,1,16,128]{3,2,1,0:T(8,128)S(1)}, u32[]{:S(2)}) copy-start(f32[32,1,16,128]{3,2,1,0:T(8,128)S(1)} %collective-permute-done.12) | copy-start | bytes 786436
  458.7 2.6 collective-permute-start.15
  460.0 3.1 collective-permute-start.14
  463.1 303.7 %copy-start.12 = (f32[32,4,1,128]{3,2,1,0:T(1,128)}, f32[32,4,1,128]{3,2,1,0:T(1,128)S(1)}, u32[]{:S(2)}) copy-start(f32[32,4,1,128]{3,2,1,0:T(1,128)S(1)} %collective-permute-done.14) | copy-start | bytes 196612
  502.9 263.9 %copy-start.22 = (f32[2,16,128]{2,1,0:T(8,128)S(1)}, f32[2,16,128]{2,1,0:T(8,128)}, u32[]{:S(2)}) copy-start(f32[2,16,128]{2,1,0:T(8,128)} %copy-done.21) | copy-start | bytes 49156
  502.9 263.9 %copy-start.24 = (f32[2,16,128]{2,1,0:T(8,128)S(1)}, f32[2,16,128]{2,1,0:T(8,128)}, u32[]{:S(2)}) copy-start(f32[2,16,128]{2,1,0:T(8,128)} %copy-done.23) | copy-start | bytes 49156
  769.1 7.3 collective-permute-start.17
  771.8 12.9 %collective-permute-start.16 = (f32[32,1,16,128]{3,2,1,0:T(8,128)S(1)}, f32[32,1,16,128]{3,2,1,0:T(8,128)S(1)}, u32[]{:S(2)}, u32[]{:S(2)}) collective-permute-start(f32[32,1,16,128]{3,2,1,0:T(8,128)S(1)} %get-tuple-element.298), channel_id=1, source_target_pairs={{2,0},{4,2},{6,4},{8,6},{10,8},{12,10},{14,12},{16,14},{18,16},{20... | collective-permute-start | bytes 786440 | tf_op jit(solution)/shard_map/ppermute | solution.py:25
  784.7 10.9 %collective-permute-start.19 = (f32[32,4,1,128]{3,2,1,0:T(1,128)S(1)}, f32[32,4,1,128]{3,2,1,0:T(1,128)S(1)}, u32[]{:S(2)}, u32[]{:S(2)}) collective-permute-start(f32[32,4,1,128]{3,2,1,0:T(1,128)S(1)} %get-tuple-element.279), channel_id=1, source_target_pairs={{0,1},{2,3},{4,5},{6,7},{8,9},{10,11},{12,13},{14,15},{16,17},{18,... | collective-permute-start | bytes 196616 | tf_op jit(solution)/shard_map/ppermute | solution.py:22
  786.0 9.6 %collective-permute-start.18 = (f32[32,4,1,128]{3,2,1,0:T(1,128)S(1)}, f32[32,4,1,128]{3,2,1,0:T(1,128)S(1)}, u32[]{:S(2)}, u32[]{:S(2)}) collective-permute-start(f32[32,4,1,128]{3,2,1,0:T(1,128)S(1)} %get-tuple-element.280), channel_id=1, source_target_pairs={{1,0},{3,2},{5,4},{7,6},{9,8},{11,10},{13,12},{15,14},{17,16},{19,... | collective-permute-start | bytes 196616 | tf_op jit(solution)/shard_map/ppermute | solution.py:25
  790.4 12.6 %all-to-all-start.3 = ((f32[16,1,128]{2,1,0:T(1,128)}), f32[16,1,128]{2,1,0:T(1,128)S(1)}, u32[]{:S(2)}, u32[]{:S(2)}) async-start(f32[16,1,128]{2,1,0:T(1,128)} %bitcast.16), calls=%async_computation.5 | async-start | bytes 16384 | tf_op jit(solution)/shard_map/all_to_all | solution.py:169
  811.5 13.7 %collective-permute-start.21 = (f32[32,1,16,128]{3,2,1,0:T(8,128)S(1)}, f32[32,1,16,128]{3,2,1,0:T(8,128)S(1)}, u32[]{:S(2)}, u32[]{:S(2)}) collective-permute-start(f32[32,1,16,128]{3,2,1,0:T(8,128)S(1)} %get-tuple-element.289), channel_id=1, source_target_pairs={{0,2},{2,4},{4,6},{6,8},{8,10},{10,12},{12,14},{14,16},{16,18},{18... | collective-permute-start | bytes 786440 | tf_op jit(solution)/shard_map/ppermute | solution.py:22
  814.2 12.9 %collective-permute-start.20 = (f32[32,1,16,128]{3,2,1,0:T(8,128)S(1)}, f32[32,1,16,128]{3,2,1,0:T(8,128)S(1)}, u32[]{:S(2)}, u32[]{:S(2)}) collective-permute-start(f32[32,1,16,128]{3,2,1,0:T(8,128)S(1)} %get-tuple-element.290), channel_id=1, source_target_pairs={{2,0},{4,2},{6,4},{8,6},{10,8},{12,10},{14,12},{16,14},{18,16},{20... | collective-permute-start | bytes 786440 | tf_op jit(solution)/shard_map/ppermute | solution.py:25
  827.2 2.6 collective-permute-start.23
  828.5 3.1 collective-permute-start.22
  (15 other events, 218.1 us)
Sparse Core Ops, SparseCore 0:
  30.5 59.5 all-gather.2
  354.1 6.7 reduce-scatter.2
  443.2 59.7 all-gather.4
  766.9 6.6 reduce-scatter.4
where the time goes:
time: 851 us; the launch traced here: 842 us
  matrix products  469 us (55%)
  waiting for transfers between devices  161 us (19%)
  local copies, waits for them, and re-layouts  77.9 us (9%)
  starting transfers between devices  50.7 us (6%)
  other arithmetic  42.4 us (5%)
  blocking collectives  26.8 us (3%)
  between operations  14.6 us (2%)
    dot_general x64, matrix products, one_step(): jnp.einsum('en,tn->et', segment, kernel, preferred_element_type=jnp.float32)  464 us
    all_gather x2, waiting for transfers between devices, per_device(): block_piece = lax.all_gather(density, 'vol', axis=1, tiled=True)  73.3 us
    slice x128, local copies, waits for them, and re-layouts, one_step(): offset = target_points[component][:, None] - places[component][None, :]  61.3 us
    ppermute x12, waiting for transfers between devices, extended(): lax.ppermute(lax.slice_in_dim(block, block.shape[dim] - width, None, axis...  43.5 us
    ppermute x12, waiting for transfers between devices, extended(): lax.ppermute(lax.slice_in_dim(block, 0, width, axis=dim), axis, backward)  31.6 us
    all_to_all x2, blocking collectives, per_device(): lax.all_to_all(outgoing, 'vol', split_axis=0, concat_axis=0, tiled=True)  26.8 us
    ppermute x12, starting transfers between devices, extended(): lax.ppermute(lax.slice_in_dim(block, block.shape[dim] - width, None, axis...  24.2 us
  transfers between devices with their start and end apart: 30, of which 20 were waited for; matrix products, arithmetic and copies ran while one was open for 3% of the time, Pallas kernels for 0%

commit v1 on v0

--- a/solution.py
+++ b/solution.py
@@ -82,6 +82,14 @@
     for weight, neighbour in zip(weights, neighbours):
         applied = applied - weight * neighbour
     return center + RELAXATION * (forcing - applied) / diagonal
+
+
+def kernel_block(targets, places):
+    dist_sq = jnp.zeros((targets.shape[1], places.shape[1]), jnp.float32)
+    for component in range(3):
+        offset = targets[component][:, None] - places[component][None, :]
+        dist_sq = dist_sq + offset * offset
+    return lax.rsqrt(dist_sq + SOFTENING * SOFTENING).astype(jnp.bfloat16)
 
 
 def with_rim(potential):
@@ -115,9 +123,24 @@
     slot_rank = jnp.arange(slot_count, dtype=jnp.int32) % capacity
     live_count = jnp.repeat(face_count.reshape(-1), capacity, total_repeat_length=slot_count)
     slot_scale = jnp.where(slot_rank < live_count, face_weight.reshape(-1), 0.0)
-    owner_table = (
-        slot_panel.reshape(-1)[:, None] == jnp.arange(piece_len, dtype=jnp.int32)[None, :]
-    ).astype(jnp.float32)
+    compact = slot_count < piece_len
+    vol_index = lax.axis_index("vol")
+    src_index = lax.axis_index("src")
+    src_count = lax.axis_size("src")
+    panels = slot_panel.reshape(-1)
+    if compact:
+        own_points = jnp.concatenate(
+            [
+                jnp.take(lax.dynamic_slice_in_dim(source_points, vol_index * piece_len, piece_len, 1), panels, axis=1),
+                jnp.take(lax.dynamic_slice_in_dim(target_points, src_index * piece_len, piece_len, 1), panels, axis=1),
+                panels.astype(jnp.float32)[None],
+            ]
+        )
+        own_targets = lax.dynamic_slice_in_dim(target_points, src_index * piece_len, piece_len, 1)
+    else:
+        owner_table = (
+            panels[:, None] == jnp.arange(piece_len, dtype=jnp.int32)[None, :]
+        ).astype(jnp.float32)
     flux_scale = float(P_SIZE) ** (-0.5)
     potential = start
     flux_own = jnp.zeros((exc_count, piece_len), jnp.float32)
@@ -128,51 +151,90 @@
         weights = face_weights(nu_ext, domain_edges)
         diagonal = weights[0] + weights[1] + weights[2] + weights[3] + weights[4] + weights[5]
         cell_values = jnp.take(potential.reshape(exc_count, cell_count), slot_cells, axis=1)
-        outgoing = (cell_values * slot_scale[None, :]).T.reshape(vol_count, capacity * exc_count)
-        arrived = lax.all_to_all(outgoing, "vol", split_axis=0, concat_axis=0, tiled=True).reshape(
-            slot_count, exc_count
-        )
-        density = jnp.dot(
-            arrived.T,
-            owner_table,
-            precision=lax.Precision.HIGHEST,
-            preferred_element_type=jnp.float32,
-        ).astype(jnp.bfloat16)
-        block_piece = lax.all_gather(density, "vol", axis=1, tiled=True)
-        piece_count = block_piece.shape[1]
-        step_len = 1024
-
-        def one_step(step_index, partial_value):
-            offset_index = step_index * step_len
-            segment = lax.dynamic_slice_in_dim(block_piece, offset_index, step_len, 1)
-            places = lax.dynamic_slice_in_dim(source_points, offset_index, step_len, 1)
-            dist_sq = jnp.zeros((target_len, step_len), jnp.float32)
-            for component in range(3):
-                offset = target_points[component][:, None] - places[component][None, :]
-                dist_sq = dist_sq + offset * offset
-            kernel = lax.rsqrt(dist_sq + SOFTENING * SOFTENING).astype(jnp.bfloat16)
-            return partial_value + jnp.einsum(
-                "en,tn->et", segment, kernel, preferred_element_type=jnp.float32
-            )
-
-        partial_flux = lax.fori_loop(
-            0, piece_count // step_len, one_step, jnp.zeros((exc_count, target_len), jnp.float32)
-        )
-        flux_sum = lax.psum_scatter(partial_flux, "src", scatter_dimension=1, tiled=True)
-        flux_own = flux_sum * flux_scale
-        per_slot = jnp.dot(
-            flux_own,
-            owner_table.T,
-            precision=lax.Precision.HIGHEST,
-            preferred_element_type=jnp.float32,
-        )
-        returned = lax.all_to_all(
-            per_slot.T.reshape(vol_count, capacity * exc_count),
-            "vol",
-            split_axis=0,
-            concat_axis=0,
-            tiled=True,
-        ).reshape(slot_count, exc_count)
+        if compact:
+            traces = (cell_values * slot_scale[None, :]).T
+            message = traces if outer_index else jnp.concatenate([traces, own_points.T], axis=1)
+            gathered = lax.all_gather(message, ("vol", "src"), axis=0, tiled=False)
+            gathered = gathered.reshape(vol_count, src_count, slot_count, -1)
+            if outer_index == 0:
+                points = gathered[..., exc_count:]
+                places = points[..., :3].reshape(-1, 3).T
+                ids = points[..., 6]
+                same = ids[..., :, None] == ids[..., None, :]
+                rank = jnp.arange(slot_count)
+                earlier = same & (rank[None, :] < rank[:, None])
+                merge = (same & ~jnp.any(earlier, axis=-1)[..., None]).astype(jnp.float32)
+                mine = lax.dynamic_index_in_dim(points, src_index, 1, keepdims=False)
+                mine = mine.reshape(vol_count, vol_count, capacity, -1)
+                mine = lax.dynamic_index_in_dim(mine, vol_index, 1, keepdims=False)
+                slot_targets = mine[..., 3:6].reshape(-1, 3).T
+                slot_kernel = kernel_block(slot_targets, places)
+            arrived = gathered[..., :exc_count].reshape(
+                vol_count, src_count, vol_count, capacity, exc_count
+            )
+            arrived = arrived.transpose(2, 1, 0, 3, 4).reshape(
+                vol_count, src_count, slot_count, exc_count
+            )
+            density = jnp.einsum(
+                "wsij,wsje->wsie", merge, arrived, precision=lax.Precision.HIGHEST
+            )
+            density = density.reshape(-1, exc_count).astype(jnp.bfloat16)
+            returned = flux_scale * jnp.einsum(
+                "tn,ne->te", slot_kernel, density, preferred_element_type=jnp.float32
+            )
+            if outer_index == ITERS - 1:
+                flux_own = flux_scale * jnp.einsum(
+                    "ne,tn->et",
+                    density,
+                    kernel_block(own_targets, places),
+                    preferred_element_type=jnp.float32,
+                )
+        else:
+            outgoing = (cell_values * slot_scale[None, :]).T.reshape(vol_count, capacity * exc_count)
+            arrived = lax.all_to_all(outgoing, "vol", split_axis=0, concat_axis=0, tiled=True).reshape(
+                slot_count, exc_count
+            )
+            density = jnp.dot(
+                arrived.T,
+                owner_table,
+                precision=lax.Precision.HIGHEST,
+                preferred_element_type=jnp.float32,
+            ).astype(jnp.bfloat16)
+            block_piece = lax.all_gather(density, "vol", axis=1, tiled=True)
+            piece_count = block_piece.shape[1]
+            step_len = 1024
+
+            def one_step(step_index, partial_value):
+                offset_index = step_index * step_len
+                segment = lax.dynamic_slice_in_dim(block_piece, offset_index, step_len, 1)
+                places = lax.dynamic_slice_in_dim(source_points, offset_index, step_len, 1)
+                dist_sq = jnp.zeros((target_len, step_len), jnp.float32)
+                for component in range(3):
+                    offset = target_points[component][:, None] - places[component][None, :]
+                    dist_sq = dist_sq + offset * offset
+                kernel = lax.rsqrt(dist_sq + SOFTENING * SOFTENING).astype(jnp.bfloat16)
+                return partial_value + jnp.einsum(
+                    "en,tn->et", segment, kernel, preferred_element_type=jnp.float32
+                )
+
+            partial_flux = lax.fori_loop(
+                0, piece_count // step_len, one_step, jnp.zeros((exc_count, target_len), jnp.float32)
+            )
+            flux_sum = lax.psum_scatter(partial_flux, "src", scatter_dimension=1, tiled=True)
+            flux_own = flux_sum * flux_scale
+            per_slot = jnp.dot(
+                flux_own,
+                owner_table.T,
+                precision=lax.Precision.HIGHEST,
+                preferred_element_type=jnp.float32,
+            )
+            returned = lax.all_to_all(
+                per_slot.T.reshape(vol_count, capacity * exc_count),
+                "vol",
+                split_axis=0,
+                concat_axis=0,
+                tiled=True,
+            ).reshape(slot_count, exc_count)
         contribution = returned.T * slot_scale[None, :]
         surface = (
             jnp.zeros((exc_count, cell_count), jnp.float32).at[:, slot_cells].add(contribution)

time: 851 us -> 259 us (0.30)
  matrix products: 469 us -> 12.4 us
  waiting for transfers between devices: 161 us -> 47.3 us
  blocking collectives: 26.8 us -> 85.4 us
  local copies, waits for them, and re-layouts: 77.9 us -> 30.2 us
  between operations: 14.6 us -> 1.77 us
  other arithmetic: 42.4 us -> 31 us
    dot_general x68 -> x5, matrix products: 469 us -> 12.4 us  [the longest x1 6.9 us: per_device(): jnp.einsum('ne,tn->et', density, kernel_block(own_targets, places), prefe...]
    all_gather x0 -> x2, blocking collectives: none -> 85.4 us  [per_device(): gathered = lax.all_gather(message, ('vol', 'src'), axis=0, tiled=False)]
    all_gather x2 -> x0, waiting for transfers between devices: 73.3 us -> none  [per_device(): block_piece = lax.all_gather(density, 'vol', axis=1, tiled=True)]
    slice x128 -> x11, local copies, waits for them, and re-layouts: 61.3 us -> 2.19 us  [the longest x2 1.46 us: kernel_block(): offset = targets[component][:, None] - places[component][None, :]]
    all_to_all x2 -> x0, blocking collectives: 26.8 us -> none  [per_device(): lax.all_to_all(outgoing, 'vol', split_axis=0, concat_axis=0, tiled=True)]
    ppermute x12, waiting for transfers between devices: 31.6 us -> 8.57 us  [extended(): lax.ppermute(lax.slice_in_dim(block, 0, width, axis=dim), axis, backward)]
    all_to_all x2 -> x0, waiting for transfers between devices: 12.2 us -> none  [per_device(): lax.all_to_all(per_slot.T.reshape(vol_count, capacity * exc_count), 'vol'...]
    all_to_all x2 -> x0, starting transfers between devices: 10.7 us -> none  [per_device(): lax.all_to_all(per_slot.T.reshape(vol_count, capacity * exc_count), 'vol'...]
  transfers between devices with their start and end apart: 30 -> 24, of which waited for: 20 -> 11; matrix products, arithmetic and copies ran while one was open for 3% -> 18% of each run, Pallas kernels for 0% -> 0%
where the time goes in v1:
time: 259 us; the launch traced here: 257 us
  blocking collectives  85.4 us (33%)
  starting transfers between devices  48.7 us (19%)
  waiting for transfers between devices  47.3 us (18%)
  other arithmetic  31 us (12%)
  local copies, waits for them, and re-layouts  30.2 us (12%)
  matrix products  12.4 us (5%)
    all_gather x2, blocking collectives, per_device(): gathered = lax.all_gather(message, ('vol', 'src'), axis=0, tiled=False)  85.4 us
    ppermute x12, waiting for transfers between devices, extended(): lax.ppermute(lax.slice_in_dim(block, block.shape[dim] - width, None, axis...  38.7 us
    ppermute x12, starting transfers between devices, extended(): lax.ppermute(lax.slice_in_dim(block, block.shape[dim] - width, None, axis...  32.8 us
    ppermute x12, starting transfers between devices, extended(): lax.ppermute(lax.slice_in_dim(block, 0, width, axis=dim), axis, backward)  15.9 us
    concatenate x9, other arithmetic, extended(): block = jnp.concatenate([low, block, high], axis=dim)  10.4 us
    ppermute x12, waiting for transfers between devices, extended(): lax.ppermute(lax.slice_in_dim(block, 0, width, axis=dim), axis, backward)  8.57 us
    add x4, other arithmetic, relax(): return center + RELAXATION * (forcing - applied) / diagonal  7.3 us
    dot_general x1, matrix products, per_device(): jnp.einsum('ne,tn->et', density, kernel_block(own_targets, places), prefe...  6.9 us
  transfers between devices with their start and end apart: 24, of which 11 were waited for; matrix products, arithmetic and copies ran while one was open for 18% of the time, Pallas kernels for 0%

profile of v1, /device:TPU:0, one launch (start us, length us, event | category | flops | bytes accessed | tf_op | source)
XLA Modules:
  0.0 256.7 jit_solution(5623796821892055032)
XLA Ops:
  0.7 1.9 fusion.84
  3.9 6.2 %collective-permute-start.1 = (f32[32,1,16,128]{3,2,1,0:T(8,128)}, f32[32,1,16,128]{3,2,1,0:T(8,128)}, u32[]{:S(2)}, u32[]{:S(2)}) collective-permute-start(f32[32,1,16,128]{3,2,1,0:T(8,128)} %get-tuple-element.60), channel_id=1, source_target_pairs={{0,2},{2,4},{4,6},{6,8},{8,10},{10,12},{12,14},{14,16},{16,18},{18... | collective-permute-start | bytes 786440 | tf_op jit(solution)/shard_map/ppermute | solution.py:22
  12.1 3.0 %copy.115 = f32[32,2,16,128]{0,3,2,1:T(8,128)} copy(f32[32,2,16,128]{3,2,1,0:T(8,128)} %param.16) | data formatting | bytes 1048576 | tf_op args[1]
  18.1 2.2 gather_fusion.1
  20.7 41.3 %all-gather.2 = f32[32,64,39]{1,2,0:T(8,128)S(1)} all-gather(f32[1,64,39]{1,2,0:T(8,128)S(1)} %copy.119), channel_id=2, replica_groups=mesh['vol'=16,'src'=2] {'vol','src'}, dimensions={0}, use_global_device_ids=true | all-gather | bytes 329472 | tf_op jit(solution)/shard_map/all_gather | solution.py:157
  65.0 2.1 convolution_convert_fusion.1
  71.0 2.2 collective-permute-start.3
  75.8 1.4 copy.130
  77.2 2.5 scatter_custom_fusion
  79.6 3.0 %copy.131 = f32[32,2,16,128]{3,2,1,0:T(8,128)} copy(f32[32,2,16,128]{0,3,2,1:T(8,128)} %bitcast.87) | data formatting | bytes 1048576 | tf_op jit(solution)/shard_map/reshape | solution.py:242
  82.7 1.4 select_maximum_fusion.12
  84.1 1.5 divide_add_fusion.3
  85.7 1.4 collective-permute-start.5
  88.7 10.4 %collective-permute-done.5 = f32[32,1,16,128]{3,2,1,0:T(8,128)S(1)} collective-permute-done((f32[32,1,16,128]{3,2,1,0:T(8,128)S(1)}, f32[32,1,16,128]{3,2,1,0:T(8,128)S(1)}, u32[]{:S(2)}, u32[]{:S(2)}) %collective-permute-start.5) | collective-permute-done | bytes 262176 | tf_op jit(solution)/shard_map/ppermute | solution.py:22
  99.8 2.0 collective-permute-start.7
  103.2 1.8 collective-permute-done.6
  105.1 2.2 divide_add_fusion.2
  107.3 3.9 %collective-permute-start.9 = (f32[32,1,16,128]{3,2,1,0:T(8,128)S(1)}, f32[32,1,16,128]{3,2,1,0:T(8,128)S(1)}, u32[]{:S(2)}, u32[]{:S(2)}) collective-permute-start(f32[32,1,16,128]{3,2,1,0:T(8,128)S(1)} %get-tuple-element.49), channel_id=1, source_target_pairs={{0,2},{2,4},{4,6},{6,8},{8,10},{10,12},{12,14},{14,16},{16,18},{18... | collective-permute-start | bytes 786440 | tf_op jit(solution)/shard_map/ppermute | solution.py:22
  111.1 1.5 collective-permute-start.8
  112.6 10.0 %collective-permute-done.9 = f32[32,1,16,128]{3,2,1,0:T(8,128)S(1)} collective-permute-done((f32[32,1,16,128]{3,2,1,0:T(8,128)S(1)}, f32[32,1,16,128]{3,2,1,0:T(8,128)S(1)}, u32[]{:S(2)}, u32[]{:S(2)}) %collective-permute-start.9) | collective-permute-done | bytes 262176 | tf_op jit(solution)/shard_map/ppermute | solution.py:22
  123.5 1.6 collective-permute-start.11
  126.3 1.8 collective-permute-done.10
  128.2 2.2 select_maximum_fusion.8
  132.4 2.0 copy.132
  134.4 3.8 %collective-permute-start.13 = (f32[32,1,16,128]{3,2,1,0:T(8,128)}, f32[32,1,16,128]{3,2,1,0:T(8,128)S(1)}, u32[]{:S(2)}, u32[]{:S(2)}) collective-permute-start(f32[32,1,16,128]{3,2,1,0:T(8,128)} %get-tuple-element.47), channel_id=1, source_target_pairs={{0,2},{2,4},{4,6},{6,8},{8,10},{10,12},{12,14},{14,16},{16,18},{18... | collective-permute-start | bytes 786440 | tf_op jit(solution)/shard_map/ppermute | solution.py:22
  139.5 2.3 gather_fusion.4
  141.9 44.1 %all-gather.3 = f32[32,64,32]{1,2,0:T(8,128)} all-gather(f32[1,64,32]{1,2,0:T(8,128)S(1)} %copy.133), channel_id=3, replica_groups=mesh['vol'=16,'src'=2] {'vol','src'}, dimensions={0}, use_global_device_ids=true | all-gather | bytes 270336 | tf_op jit(solution)/shard_map/all_gather | solution.py:157
  186.0 1.4 copy.134
  187.6 2.1 convolution_convert_fusion
  191.2 2.3 collective-permute-start.15
  195.3 2.4 scatter_custom_fusion.1
  197.7 2.3 copy.139
  200.0 3.1 %select_maximum_fusion.4 = f32[32,4,18,130]{3,2,1,0:T(8,128)S(1)} fusion(f32[32,4,1,128]{3,2,1,0:T(1,128)S(1)} %collective-permute-done.14, f32[32,4,1,128]{3,2,1,0:T(1,128)S(1)} %collective-permute-done.15, f32[32,1,16,128]{3,2,1,0:T(8,128)} %collective-permute-done.12, f32[32,2,16,128]{3,2,1,0:T(8,128)S(1)} %fusion.42, ...), kind=kLoop, calls=%fused_computation.15 | loop fusion | flops 3594240 | bytes 2377728 | tf_op jit(solution)/shard_map/concatenate | solution.py:26
  203.2 1.5 divide_add_fusion.1
  204.7 1.8 collective-permute-start.17
  208.0 10.6 %collective-permute-done.17 = f32[32,1,16,128]{3,2,1,0:T(8,128)S(1)} collective-permute-done((f32[32,1,16,128]{3,2,1,0:T(8,128)S(1)}, f32[32,1,16,128]{3,2,1,0:T(8,128)S(1)}, u32[]{:S(2)}, u32[]{:S(2)}) %collective-permute-start.17) | collective-permute-done | bytes 262176 | tf_op jit(solution)/shard_map/ppermute | solution.py:22
  219.0 2.1 collective-permute-start.19
  222.4 1.8 collective-permute-done.18
  224.3 2.1 divide_add_fusion
  226.4 4.1 %collective-permute-start.21 = (f32[32,1,16,128]{3,2,1,0:T(8,128)S(1)}, f32[32,1,16,128]{3,2,1,0:T(8,128)S(1)}, u32[]{:S(2)}, u32[]{:S(2)}) collective-permute-start(f32[32,1,16,128]{3,2,1,0:T(8,128)S(1)} %get-tuple-element.37), channel_id=1, source_target_pairs={{0,2},{2,4},{4,6},{6,8},{8,10},{10,12},{12,14},{14,16},{16,18},{18... | collective-permute-start | bytes 786440 | tf_op jit(solution)/shard_map/ppermute | solution.py:22
  230.5 1.5 collective-permute-start.20
  232.0 1.4 slice_reduce_fusion.2
  233.5 7.7 %collective-permute-done.21 = f32[32,1,16,128]{3,2,1,0:T(8,128)S(1)} collective-permute-done((f32[32,1,16,128]{3,2,1,0:T(8,128)S(1)}, f32[32,1,16,128]{3,2,1,0:T(8,128)S(1)}, u32[]{:S(2)}, u32[]{:S(2)}) %collective-permute-start.21) | collective-permute-done | bytes 262176 | tf_op jit(solution)/shard_map/ppermute | solution.py:22
  241.1 1.6 collective-permute-done.20
  242.8 1.6 collective-permute-start.23
  245.7 6.9 %fusion.2 = f32[32,2048]{1,0:T(8,128)} fusion(bf16[2048,32]{0,1:T(8,128)(2,1)S(1)} %convert_element_type.45, f32[2048]{0:T(1024)S(1)} %bitcast.106, f32[2048]{0:T(1024)S(1)} %get-tuple-element.17, f32[2048]{0:T(1024)S(1)} %bitcast.109, f32[2048]{0:T(1024)S(1)} %get-tuple-element.18, f32[2048]{0:T(1024)S(1)} %bitcast.103, f32[2048]{0:T(1024)S(1)} %get-tuple-element.16), kind=kOutput, calls=%fused_computation.26 | convolution fusion | flops 310444032 | bytes 442368 | tf_op jit(solution)/shard_map/ne,tn->et/dot_general | solution.py:186
  252.6 2.2 select_maximum_fusion
  254.8 1.9 fusion.16
  (170 shorter events, 33.1 us)
Async XLA Ops:
  0.6 15.0 %copy-start = (f32[3,32768]{1,0:T(4,128)S(1)}, f32[3,32768]{1,0:T(4,128)}, u32[]{:S(2)}) copy-start(f32[3,32768]{1,0:T(4,128)} %param.23) | copy-start | bytes 1179652
  0.6 14.5 %copy-start.25 = (s32[64]{0:T(128)S(1)}, s32[64]{0:T(128)}, u32[]{:S(2)}) copy-start(s32[64]{0:T(128)} %constant.189) | copy-start | bytes 772
  0.7 14.6 %copy-start.11 = (f32[3,4096]{1,0:T(4,128)S(1)}, f32[3,4096]{1,0:T(4,128)}, u32[]{:S(2)}) copy-start(f32[3,4096]{1,0:T(4,128)} %param.22) | copy-start | bytes 147460
  0.7 16.6 %copy-start.1 = (s32[1,1,16]{2,1,0:T(1,128)S(1)}, s32[1,1,16]{2,1,0:T(1,128)}, u32[]{:S(2)}) copy-start(s32[1,1,16]{2,1,0:T(1,128)} %param.19) | copy-start | bytes 196
  0.7 17.4 %copy-start.26 = (f32[1,1,64]{2,1,0:T(1,128)S(1)}, f32[1,1,64]{2,1,0:T(1,128)}, u32[]{:S(2)}) copy-start(f32[1,1,64]{2,1,0:T(1,128)} %param.20) | copy-start | bytes 772
  2.6 67.6 %collective-permute-start = (f32[32,1,16,128]{3,2,1,0:T(8,128)}, f32[32,1,16,128]{3,2,1,0:T(8,128)S(1)}, u32[]{:S(2)}, u32[]{:S(2)}) collective-permute-start(f32[32,1,16,128]{3,2,1,0:T(8,128)} %get-tuple-element.59), channel_id=1, source_target_pairs={{2,0},{4,2},{6,4},{8,6},{10,8},{12,10},{14,12},{16,14},{18,16},{20... | collective-permute-start | bytes 786440 | tf_op jit(solution)/shard_map/ppermute | solution.py:25
  3.9 65.3 %collective-permute-start.1 = (f32[32,1,16,128]{3,2,1,0:T(8,128)}, f32[32,1,16,128]{3,2,1,0:T(8,128)}, u32[]{:S(2)}, u32[]{:S(2)}) collective-permute-start(f32[32,1,16,128]{3,2,1,0:T(8,128)} %get-tuple-element.60), channel_id=1, source_target_pairs={{0,2},{2,4},{4,6},{6,8},{8,10},{10,12},{12,14},{14,16},{16,18},{18... | collective-permute-start | bytes 786440 | tf_op jit(solution)/shard_map/ppermute | solution.py:22
  11.4 50.6 %copy-start.21 = (pred[64]{0:T(512)(128)(4,1)}, pred[64]{0:T(512)(128)(4,1)S(1)}, u32[]{:S(2)}) copy-start(pred[64]{0:T(512)(128)(4,1)S(1)} %get-tuple-element.74) | copy-start | bytes 196
  15.1 47.0 %copy-start.20 = (s32[1024]{0:T(1024)}, s32[1024]{0:T(1024)S(1)}, u32[]{:S(2)}) copy-start(s32[1024]{0:T(1024)S(1)} %pad_clamp_fusion.2) | copy-start | bytes 12292
  18.0 44.1 %copy-start.23 = (f32[64]{0:T(128)}, f32[64]{0:T(128)S(1)}, u32[]{:S(2)}) copy-start(f32[64]{0:T(128)S(1)} %get-tuple-element.24) | copy-start | bytes 772
  18.0 49.5 %copy-start.27 = (f32[64]{0:T(128)}, f32[64]{0:T(128)S(1)}, u32[]{:S(2)}) copy-start(f32[64]{0:T(128)S(1)} %get-tuple-element.23) | copy-start | bytes 772
  64.3 5.9 %copy-start.2 = (f32[32,2,16,128]{3,2,1,0:T(8,128)S(1)}, f32[32,2,16,128]{3,2,1,0:T(8,128)}, u32[]{:S(2)}) copy-start(f32[32,2,16,128]{3,2,1,0:T(8,128)} %param.16) | copy-start | bytes 1572868
  71.0 11.6 %collective-permute-start.3 = (f32[32,4,1,128]{3,2,1,0:T(1,128)}, f32[32,4,1,128]{3,2,1,0:T(1,128)S(1)}, u32[]{:S(2)}, u32[]{:S(2)}) collective-permute-start(f32[32,4,1,128]{3,2,1,0:T(1,128)} %get-tuple-element.35), channel_id=1, source_target_pairs={{0,1},{2,3},{4,5},{6,7},{8,9},{10,11},{12,13},{14,15},{16,17},{18,... | collective-permute-start | bytes 196616 | tf_op jit(solution)/shard_map/ppermute | solution.py:22
  73.3 9.4 %collective-permute-start.2 = (f32[32,4,1,128]{3,2,1,0:T(1,128)}, f32[32,4,1,128]{3,2,1,0:T(1,128)S(1)}, u32[]{:S(2)}, u32[]{:S(2)}) collective-permute-start(f32[32,4,1,128]{3,2,1,0:T(1,128)} %get-tuple-element.36), channel_id=1, source_target_pairs={{1,0},{3,2},{5,4},{7,6},{9,8},{11,10},{13,12},{15,14},{17,16},{19,... | collective-permute-start | bytes 196616 | tf_op jit(solution)/shard_map/ppermute | solution.py:25
  85.7 19.4 %copy-start.3 = (f32[32,2,16,128]{3,2,1,0:T(8,128)S(1)}, f32[32,2,16,128]{3,2,1,0:T(8,128)}, u32[]{:S(2)}) copy-start(f32[32,2,16,128]{3,2,1,0:T(8,128)} %param.15) | copy-start | bytes 1572868
  85.7 19.4 %copy-start.5 = (f32[32,2,16,128]{3,2,1,0:T(8,128)S(1)}, f32[32,2,16,128]{3,2,1,0:T(8,128)}, u32[]{:S(2)}) copy-start(f32[32,2,16,128]{3,2,1,0:T(8,128)} %copy.131) | copy-start | bytes 1572868
  85.7 13.4 %collective-permute-start.5 = (f32[32,1,16,128]{3,2,1,0:T(8,128)S(1)}, f32[32,1,16,128]{3,2,1,0:T(8,128)S(1)}, u32[]{:S(2)}, u32[]{:S(2)}) collective-permute-start(f32[32,1,16,128]{3,2,1,0:T(8,128)S(1)} %get-tuple-element.57), channel_id=1, source_target_pairs={{0,2},{2,4},{4,6},{6,8},{8,10},{10,12},{12,14},{14,16},{16,18},{18... | collective-permute-start | bytes 786440 | tf_op jit(solution)/shard_map/ppermute | solution.py:22
  87.2 12.5 %collective-permute-start.4 = (f32[32,1,16,128]{3,2,1,0:T(8,128)S(1)}, f32[32,1,16,128]{3,2,1,0:T(8,128)S(1)}, u32[]{:S(2)}, u32[]{:S(2)}) collective-permute-start(f32[32,1,16,128]{3,2,1,0:T(8,128)S(1)} %get-tuple-element.58), channel_id=1, source_target_pairs={{2,0},{4,2},{6,4},{8,6},{10,8},{12,10},{14,12},{16,14},{18,16},{20... | collective-permute-start | bytes 786440 | tf_op jit(solution)/shard_map/ppermute | solution.py:25
  99.8 3.4 %collective-permute-start.7 = (f32[32,4,1,128]{3,2,1,0:T(1,128)S(1)}, f32[32,4,1,128]{3,2,1,0:T(1,128)S(1)}, u32[]{:S(2)}, u32[]{:S(2)}) collective-permute-start(f32[32,4,1,128]{3,2,1,0:T(1,128)S(1)} %get-tuple-element.33), channel_id=1, source_target_pairs={{0,1},{2,3},{4,5},{6,7},{8,9},{10,11},{12,13},{14,15},{16,17},{18,... | collective-permute-start | bytes 196616 | tf_op jit(solution)/shard_map/ppermute | solution.py:22
  101.8 3.1 %collective-permute-start.6 = (f32[32,4,1,128]{3,2,1,0:T(1,128)S(1)}, f32[32,4,1,128]{3,2,1,0:T(1,128)S(1)}, u32[]{:S(2)}, u32[]{:S(2)}) collective-permute-start(f32[32,4,1,128]{3,2,1,0:T(1,128)S(1)} %get-tuple-element.34), channel_id=1, source_target_pairs={{1,0},{3,2},{5,4},{7,6},{9,8},{11,10},{13,12},{15,14},{17,16},{19,... | collective-permute-start | bytes 196616 | tf_op jit(solution)/shard_map/ppermute | solution.py:25
  107.3 15.3 %collective-permute-start.9 = (f32[32,1,16,128]{3,2,1,0:T(8,128)S(1)}, f32[32,1,16,128]{3,2,1,0:T(8,128)S(1)}, u32[]{:S(2)}, u32[]{:S(2)}) collective-permute-start(f32[32,1,16,128]{3,2,1,0:T(8,128)S(1)} %get-tuple-element.49), channel_id=1, source_target_pairs={{0,2},{2,4},{4,6},{6,8},{8,10},{10,12},{12,14},{14,16},{16,18},{18... | collective-permute-start | bytes 786440 | tf_op jit(solution)/shard_map/ppermute | solution.py:22
  111.1 12.2 %collective-permute-start.8 = (f32[32,1,16,128]{3,2,1,0:T(8,128)S(1)}, f32[32,1,16,128]{3,2,1,0:T(8,128)S(1)}, u32[]{:S(2)}, u32[]{:S(2)}) collective-permute-start(f32[32,1,16,128]{3,2,1,0:T(8,128)S(1)} %get-tuple-element.50), channel_id=1, source_target_pairs={{2,0},{4,2},{6,4},{8,6},{10,8},{12,10},{14,12},{16,14},{18,16},{20... | collective-permute-start | bytes 786440 | tf_op jit(solution)/shard_map/ppermute | solution.py:25
  123.5 2.9 %collective-permute-start.11 = (f32[32,4,1,128]{3,2,1,0:T(1,128)S(1)}, f32[32,4,1,128]{3,2,1,0:T(1,128)S(1)}, u32[]{:S(2)}, u32[]{:S(2)}) collective-permute-start(f32[32,4,1,128]{3,2,1,0:T(1,128)S(1)} %get-tuple-element.31), channel_id=1, source_target_pairs={{0,1},{2,3},{4,5},{6,7},{8,9},{10,11},{12,13},{14,15},{16,17},{18,... | collective-permute-start | bytes 196616 | tf_op jit(solution)/shard_map/ppermute | solution.py:22
  125.0 3.1 %collective-permute-start.10 = (f32[32,4,1,128]{3,2,1,0:T(1,128)S(1)}, f32[32,4,1,128]{3,2,1,0:T(1,128)S(1)}, u32[]{:S(2)}, u32[]{:S(2)}) collective-permute-start(f32[32,4,1,128]{3,2,1,0:T(1,128)S(1)} %get-tuple-element.32), channel_id=1, source_target_pairs={{1,0},{3,2},{5,4},{7,6},{9,8},{11,10},{13,12},{15,14},{17,16},{19,... | collective-permute-start | bytes 196616 | tf_op jit(solution)/shard_map/ppermute | solution.py:25
  131.5 10.2 %copy-start.22 = (pred[64]{0:T(512)(128)(4,1)S(1)}, pred[64]{0:T(512)(128)(4,1)}, u32[]{:S(2)}) copy-start(pred[64]{0:T(512)(128)(4,1)} %copy-done.21) | copy-start | bytes 196
  131.6 10.2 %copy-start.24 = (f32[64]{0:T(128)S(1)}, f32[64]{0:T(128)}, u32[]{:S(2)}) copy-start(f32[64]{0:T(128)} %copy-done.23) | copy-start | bytes 772
  132.4 55.2 %copy-start.9 = (f32[16,2,64]{2,1,0:T(2,128)S(1)}, f32[16,2,64]{2,1,0:T(2,128)}, u32[]{:S(2)}) copy-start(f32[16,2,64]{2,1,0:T(2,128)} %copy-done.8) | copy-start | bytes 24580
  132.4 55.2 %copy-start.13 = (pred[16,2,64]{2,1,0:T(4,128)(4,1)S(1)}, pred[16,2,64]{2,1,0:T(4,128)(4,1)}, u32[]{:S(2)}) copy-start(pred[16,2,64]{2,1,0:T(4,128)(4,1)} %copy-done.12) | copy-start | bytes 6148
  134.4 55.7 %collective-permute-start.13 = (f32[32,1,16,128]{3,2,1,0:T(8,128)}, f32[32,1,16,128]{3,2,1,0:T(8,128)S(1)}, u32[]{:S(2)}, u32[]{:S(2)}) collective-permute-start(f32[32,1,16,128]{3,2,1,0:T(8,128)} %get-tuple-element.47), channel_id=1, source_target_pairs={{0,2},{2,4},{4,6},{6,8},{8,10},{10,12},{12,14},{14,16},{16,18},{18... | collective-permute-start | bytes 786440 | tf_op jit(solution)/shard_map/ppermute | solution.py:22
  138.2 52.0 %collective-permute-start.12 = (f32[32,1,16,128]{3,2,1,0:T(8,128)}, f32[32,1,16,128]{3,2,1,0:T(8,128)}, u32[]{:S(2)}, u32[]{:S(2)}) collective-permute-start(f32[32,1,16,128]{3,2,1,0:T(8,128)} %get-tuple-element.48), channel_id=1, source_target_pairs={{2,0},{4,2},{6,4},{8,6},{10,8},{12,10},{14,12},{16,14},{18,16},{20... | collective-permute-start | bytes 786440 | tf_op jit(solution)/shard_map/ppermute | solution.py:25
  187.4 7.4 %copy-start.15 = (f32[1,2048]{1,0:T(1,128)S(1)}, f32[1,2048]{1,0:T(1,128)}, u32[]{:S(2)}) copy-start(f32[1,2048]{1,0:T(1,128)} %copy-done.14) | copy-start | bytes 24580
  187.4 7.4 %copy-start.17 = (f32[1,2048]{1,0:T(1,128)S(1)}, f32[1,2048]{1,0:T(1,128)}, u32[]{:S(2)}) copy-start(f32[1,2048]{1,0:T(1,128)} %copy-done.16) | copy-start | bytes 24580
  187.4 7.4 %copy-start.19 = (f32[1,2048]{1,0:T(1,128)S(1)}, f32[1,2048]{1,0:T(1,128)}, u32[]{:S(2)}) copy-start(f32[1,2048]{1,0:T(1,128)} %copy-done.18) | copy-start | bytes 24580
  187.4 7.4 %copy-start.28 = (f32[64]{0:T(128)S(1)}, f32[64]{0:T(128)}, u32[]{:S(2)}) copy-start(f32[64]{0:T(128)} %copy-done.27) | copy-start | bytes 772
  187.4 7.4 %copy-start.30 = (f32[64]{0:T(128)S(1)}, f32[64]{0:T(128)}, u32[]{:S(2)}) copy-start(f32[64]{0:T(128)} %copy-done.29) | copy-start | bytes 772
  187.4 7.4 %copy-start.32 = (f32[64]{0:T(128)S(1)}, f32[64]{0:T(128)}, u32[]{:S(2)}) copy-start(f32[64]{0:T(128)} %copy-done.31) | copy-start | bytes 772
  187.5 7.4 %copy-start.34 = (f32[64]{0:T(128)S(1)}, f32[64]{0:T(128)}, u32[]{:S(2)}) copy-start(f32[64]{0:T(128)} %copy-done.33) | copy-start | bytes 772
  191.2 8.8 %collective-permute-start.15 = (f32[32,4,1,128]{3,2,1,0:T(1,128)S(1)}, f32[32,4,1,128]{3,2,1,0:T(1,128)S(1)}, u32[]{:S(2)}, u32[]{:S(2)}) collective-permute-start(f32[32,4,1,128]{3,2,1,0:T(1,128)S(1)} %get-tuple-element.29), channel_id=1, source_target_pairs={{0,1},{2,3},{4,5},{6,7},{8,9},{10,11},{12,13},{14,15},{16,17},{18,... | collective-permute-start | bytes 196616 | tf_op jit(solution)/shard_map/ppermute | solution.py:22
  193.5 6.5 %collective-permute-start.14 = (f32[32,4,1,128]{3,2,1,0:T(1,128)S(1)}, f32[32,4,1,128]{3,2,1,0:T(1,128)S(1)}, u32[]{:S(2)}, u32[]{:S(2)}) collective-permute-start(f32[32,4,1,128]{3,2,1,0:T(1,128)S(1)} %get-tuple-element.30), channel_id=1, source_target_pairs={{1,0},{3,2},{5,4},{7,6},{9,8},{11,10},{13,12},{15,14},{17,16},{19,... | collective-permute-start | bytes 196616 | tf_op jit(solution)/shard_map/ppermute | solution.py:25
  204.6 19.6 %copy-start.4 = (f32[32,2,16,128]{3,2,1,0:T(8,128)S(1)}, f32[32,2,16,128]{3,2,1,0:T(8,128)}, u32[]{:S(2)}) copy-start(f32[32,2,16,128]{3,2,1,0:T(8,128)} %param.15) | copy-start | bytes 1572868
  204.7 13.9 %collective-permute-start.17 = (f32[32,1,16,128]{3,2,1,0:T(8,128)S(1)}, f32[32,1,16,128]{3,2,1,0:T(8,128)S(1)}, u32[]{:S(2)}, u32[]{:S(2)}) collective-permute-start(f32[32,1,16,128]{3,2,1,0:T(8,128)S(1)} %get-tuple-element.45), channel_id=1, source_target_pairs={{0,2},{2,4},{4,6},{6,8},{8,10},{10,12},{12,14},{14,16},{16,18},{18... | collective-permute-start | bytes 786440 | tf_op jit(solution)/shard_map/ppermute | solution.py:22
  206.5 12.4 %collective-permute-start.16 = (f32[32,1,16,128]{3,2,1,0:T(8,128)S(1)}, f32[32,1,16,128]{3,2,1,0:T(8,128)S(1)}, u32[]{:S(2)}, u32[]{:S(2)}) collective-permute-start(f32[32,1,16,128]{3,2,1,0:T(8,128)S(1)} %get-tuple-element.46), channel_id=1, source_target_pairs={{2,0},{4,2},{6,4},{8,6},{10,8},{12,10},{14,12},{16,14},{18,16},{20... | collective-permute-start | bytes 786440 | tf_op jit(solution)/shard_map/ppermute | solution.py:25
  219.0 3.5 %collective-permute-start.19 = (f32[32,4,1,128]{3,2,1,0:T(1,128)S(1)}, f32[32,4,1,128]{3,2,1,0:T(1,128)S(1)}, u32[]{:S(2)}, u32[]{:S(2)}) collective-permute-start(f32[32,4,1,128]{3,2,1,0:T(1,128)S(1)} %get-tuple-element.27), channel_id=1, source_target_pairs={{0,1},{2,3},{4,5},{6,7},{8,9},{10,11},{12,13},{14,15},{16,17},{18,... | collective-permute-start | bytes 196616 | tf_op jit(solution)/shard_map/ppermute | solution.py:22
  221.1 3.1 %collective-permute-start.18 = (f32[32,4,1,128]{3,2,1,0:T(1,128)S(1)}, f32[32,4,1,128]{3,2,1,0:T(1,128)S(1)}, u32[]{:S(2)}, u32[]{:S(2)}) collective-permute-start(f32[32,4,1,128]{3,2,1,0:T(1,128)S(1)} %get-tuple-element.28), channel_id=1, source_target_pairs={{1,0},{3,2},{5,4},{7,6},{9,8},{11,10},{13,12},{15,14},{17,16},{19,... | collective-permute-start | bytes 196616 | tf_op jit(solution)/shard_map/ppermute | solution.py:25
  226.4 14.7 %collective-permute-start.21 = (f32[32,1,16,128]{3,2,1,0:T(8,128)S(1)}, f32[32,1,16,128]{3,2,1,0:T(8,128)S(1)}, u32[]{:S(2)}, u32[]{:S(2)}) collective-permute-start(f32[32,1,16,128]{3,2,1,0:T(8,128)S(1)} %get-tuple-element.37), channel_id=1, source_target_pairs={{0,2},{2,4},{4,6},{6,8},{8,10},{10,12},{12,14},{14,16},{16,18},{18... | collective-permute-start | bytes 786440 | tf_op jit(solution)/shard_map/ppermute | solution.py:22
  230.5 12.2 %collective-permute-start.20 = (f32[32,1,16,128]{3,2,1,0:T(8,128)S(1)}, f32[32,1,16,128]{3,2,1,0:T(8,128)S(1)}, u32[]{:S(2)}, u32[]{:S(2)}) collective-permute-start(f32[32,1,16,128]{3,2,1,0:T(8,128)S(1)} %get-tuple-element.38), channel_id=1, source_target_pairs={{2,0},{4,2},{6,4},{8,6},{10,8},{12,10},{14,12},{16,14},{18,16},{20... | collective-permute-start | bytes 786440 | tf_op jit(solution)/shard_map/ppermute | solution.py:25
  242.8 9.8 %collective-permute-start.23 = (f32[32,4,1,128]{3,2,1,0:T(1,128)S(1)}, f32[32,4,1,128]{3,2,1,0:T(1,128)S(1)}, u32[]{:S(2)}, u32[]{:S(2)}) collective-permute-start(f32[32,4,1,128]{3,2,1,0:T(1,128)S(1)} %get-tuple-element.25), channel_id=1, source_target_pairs={{0,1},{2,3},{4,5},{6,7},{8,9},{10,11},{12,13},{14,15},{16,17},{18,... | collective-permute-start | bytes 196616 | tf_op jit(solution)/shard_map/ppermute | solution.py:22
  244.4 8.2 %collective-permute-start.22 = (f32[32,4,1,128]{3,2,1,0:T(1,128)S(1)}, f32[32,4,1,128]{3,2,1,0:T(1,128)S(1)}, u32[]{:S(2)}, u32[]{:S(2)}) collective-permute-start(f32[32,4,1,128]{3,2,1,0:T(1,128)S(1)} %get-tuple-element.26), channel_id=1, source_target_pairs={{1,0},{3,2},{5,4},{7,6},{9,8},{11,10},{13,12},{15,14},{17,16},{19,... | collective-permute-start | bytes 196616 | tf_op jit(solution)/shard_map/ppermute | solution.py:25
  (11 other events, 43.9 us)

commit v2 on v1

--- a/solution.py
+++ b/solution.py
@@ -1,6 +1,10 @@
+import functools
+
 import jax
 import jax.numpy as jnp
 from jax import lax
+from jax.experimental import pallas as pl
+from jax.experimental.pallas import tpu as pltpu
 from jax.sharding import PartitionSpec as P
 
 P_SIZE = 65536
@@ -94,6 +98,494 @@
 
 def with_rim(potential):
     return extended(potential, (("vol", 1), ("src", 2)), 1)
+
+
+MESH = pl.DeviceIdType.MESH
+LANES = 128
+TILE = 8
+NT = (((1,), (1,)), ((), ()))
+NN = (((1,), (0,)), ((), ()))
+
+
+def split_dot(values, selector, dims):
+    total = None
+    for _ in range(3):
+        part = values.astype(jnp.bfloat16)
+        term = lax.dot_general(part, selector, dims, preferred_element_type=jnp.float32)
+        total = term if total is None else total + term
+        values = values - part.astype(jnp.float32)
+    return total
+
+
+def pair_kernel(columns, rows):
+    dist_sq = None
+    for column, row in zip(columns, rows):
+        offset = column - row
+        dist_sq = offset * offset if dist_sq is None else dist_sq + offset * offset
+    return lax.rsqrt(dist_sq + SOFTENING * SOFTENING).astype(jnp.bfloat16)
+
+
+def fused_kernel(
+    vol_count, src_count, capacity, flux_scale,
+    start_ref, exc_ref, mat_ref, cell_ref, scale_ref, geo_ref, merge_ref, target_ref,
+    out_ref, flux_ref,
+    pe, pf, nu, forcing, a_send, ax, ay, ac, b_send, bx, by, mat_near,
+    tr_send, tr_recv, de_send, de_recv, ge_recv, ge_all, slot_kernel, dens_all,
+    halo_ss, halo_rs, tr_ss, tr_rs, de_ss, de_rs, ge_ss, ge_rs,
+):
+    width_x, width_y, exc_count, depth = start_ref.shape
+    count = vol_count * src_count
+    v, s = lax.axis_index("vol"), lax.axis_index("src")
+    me = v * src_count + s
+    group = TILE // capacity
+    slot_count = vol_count * capacity
+    first_x, last_x = v == 0, v == vol_count - 1
+    first_y, last_y = s == 0, s == src_count - 1
+
+    def device(index):
+        return (index // src_count, lax.rem(index, src_count))
+
+    barrier = pltpu.get_barrier_semaphore()
+
+    def greet(step, carry):
+        other = lax.rem(me + step, count)
+        pl.semaphore_signal(barrier, inc=1, device_id=device(other), device_id_type=MESH)
+        return carry
+
+    lax.fori_loop(1, count, greet, 0)
+
+    lane = lax.broadcasted_iota(jnp.int32, (exc_count, depth), 1)
+    at_low, at_high = lane == 0, lane == depth - 1
+    cell_row = cell_ref[0:1, :]
+    cell_depth = cell_ref[1:2, :]
+    slot_scale = scale_ref[0:1, :]
+    pick_depth = (
+        lax.broadcasted_iota(jnp.int32, (depth, LANES), 0) == cell_depth
+    ).astype(jnp.float32).astype(jnp.bfloat16)
+    chunk = 8
+
+    def traces_of(read):
+        total = jnp.zeros((exc_count, LANES), jnp.float32)
+        for x in range(width_x):
+            for y0 in range(0, width_y, chunk):
+                block = read(x, y0).reshape(chunk * exc_count, depth)
+                taken = split_dot(block, pick_depth, NN)
+                for k in range(chunk):
+                    row = x * width_y + y0 + k
+                    total = total + jnp.where(
+                        cell_row == row, taken[k * exc_count : (k + 1) * exc_count], 0.0
+                    )
+        total = total * slot_scale
+        return jnp.concatenate([total] * (LANES // exc_count), axis=0).T
+
+    def each_near(direction):
+        dv, ds = direction
+        sends, gets = True, True
+        if dv > 0:
+            sends, gets = jnp.logical_not(last_x), jnp.logical_not(first_x)
+        elif dv < 0:
+            sends, gets = jnp.logical_not(first_x), jnp.logical_not(last_x)
+        if ds > 0:
+            sends = jnp.logical_and(sends, jnp.logical_not(last_y))
+            gets = jnp.logical_and(gets, jnp.logical_not(first_y))
+        elif ds < 0:
+            sends = jnp.logical_and(sends, jnp.logical_not(first_y))
+            gets = jnp.logical_and(gets, jnp.logical_not(last_y))
+        return sends, gets
+
+    started = []
+
+    def send_near(direction, src, dst, place):
+        dv, ds = direction
+        copy = pltpu.make_async_remote_copy(
+            src_ref=src, dst_ref=dst, send_sem=halo_ss.at[place], recv_sem=halo_rs.at[place],
+            device_id=(v + dv, s + ds), device_id_type=MESH,
+        )
+        sends, gets = each_near(direction)
+        pl.when(sends)(copy.start)
+        started.append((sends, copy))
+        return gets, copy
+
+    def land(gets, copy, put, zero):
+        @pl.when(gets)
+        def _():
+            copy.wait_recv()
+            put()
+
+        pl.when(jnp.logical_not(gets))(zero)
+
+    def land_into(pair, dst, src):
+        def put():
+            dst[...] = src[...].astype(dst.dtype)
+
+        def zero():
+            dst[...] = jnp.zeros(dst.shape, dst.dtype)
+
+        land(pair[0], pair[1], put, zero)
+
+    def geo_copy(other, owner):
+        return pltpu.make_async_remote_copy(
+            src_ref=geo_ref, dst_ref=ge_recv.at[owner], send_sem=ge_ss.at[other],
+            recv_sem=ge_rs.at[owner], device_id=device(other), device_id_type=MESH,
+        )
+
+    def trace_copy(it, other, owner):
+        tile = pl.multiple_of((other // group) * TILE, TILE)
+        return pltpu.make_async_remote_copy(
+            src_ref=tr_send.at[it, pl.ds(tile, TILE)], dst_ref=tr_recv.at[it, owner],
+            send_sem=tr_ss.at[it, other], recv_sem=tr_rs.at[it, owner],
+            device_id=(other, s), device_id_type=MESH,
+        )
+
+    def density_copy(it, other, owner):
+        return pltpu.make_async_remote_copy(
+            src_ref=de_send.at[it], dst_ref=de_recv.at[it, owner], send_sem=de_ss.at[it, other],
+            recv_sem=de_rs.at[it, owner], device_id=device(other), device_id_type=MESH,
+        )
+
+    def others(total, own, body):
+        def step(index, carry):
+            body(lax.rem(own + index, total))
+            return carry
+
+        lax.fori_loop(1, total, step, 0)
+
+    def depth_near(block, low_fill, high_fill):
+        up = jnp.where(at_high, high_fill, pltpu.roll(block, depth - 1, 1))
+        down = jnp.where(at_low, low_fill, pltpu.roll(block, 1, 1))
+        return up, down
+
+    def nu_at(x, y, material):
+        center = pe[x + 2, y + 2]
+        up, down = depth_near(center, 0.0, 0.0)
+        along_x = 0.5 * (pe[x + 3, y + 2] - pe[x + 1, y + 2])
+        along_y = 0.5 * (pe[x + 2, y + 3] - pe[x + 2, y + 1])
+        along_z = 0.5 * (up - down)
+        grad_sq = along_x * along_x + along_y * along_y + along_z * along_z
+        base = jnp.zeros(material.shape, jnp.float32)
+        slope = jnp.zeros(material.shape, jnp.float32)
+        for material_id in range(3):
+            picked = material == material_id
+            base = jnp.where(picked, NU_BASE[material_id], base)
+            slope = jnp.where(picked, NU_SATURATION[material_id], slope)
+        return base + slope * grad_sq / (1.0 + grad_sq)
+
+    def all_nu():
+        def one_y(y, carry):
+            own = []
+            for x in range(width_x):
+                value = nu_at(x, y, mat_ref[x, pl.ds(y, 1), :])
+                nu[x + 1, y + 1] = value
+                own.append(value)
+            low = nu_at(-1, y, mat_near[0, width_x - 1, pl.ds(y, 1), :])
+            high = nu_at(width_x, y, mat_near[1, 0, pl.ds(y, 1), :])
+            nu[0, y + 1] = jnp.where(first_x, own[0], low)
+            nu[width_x + 1, y + 1] = jnp.where(last_x, own[-1], high)
+            return carry
+
+        lax.fori_loop(0, width_y, one_y, 0)
+        for x in range(width_x):
+            low = nu_at(x, -1, mat_near[2, x, width_y - 1 : width_y, :])
+            high = nu_at(x, width_y, mat_near[3, x, 0:1, :])
+            nu[x + 1, 0] = jnp.where(first_y, nu[x + 1, 1], low)
+            nu[x + 1, width_y + 1] = jnp.where(last_y, nu[x + 1, width_y], high)
+
+    def relaxed(read, x, y):
+        own = nu[x + 1, y + 1]
+        nu_up, nu_down = depth_near(own, own, own)
+        center = read(x, y)
+        up, down = depth_near(center, 0.0, 0.0)
+        pairs = (
+            (nu[x + 2, y + 1], read(x + 1, y)),
+            (nu[x, y + 1], read(x - 1, y)),
+            (nu[x + 1, y + 2], read(x, y + 1)),
+            (nu[x + 1, y], read(x, y - 1)),
+            (nu_up, up),
+            (nu_down, down),
+        )
+        diagonal, pulled = None, None
+        for near_nu, near in pairs:
+            weight = 0.5 * (own + near_nu)
+            diagonal = weight if diagonal is None else diagonal + weight
+            pulled = weight * near if pulled is None else pulled + weight * near
+        applied = diagonal * center - pulled
+        return center + RELAXATION * (forcing[x, y] - applied) / diagonal
+
+    def sweep(read, write):
+        def one_y(y, carry):
+            for x in range(width_x):
+                write(x, y, relaxed(read, x, y))
+            return carry
+
+        lax.fori_loop(0, width_y, one_y, 0)
+
+    def keep_start(y, carry):
+        for x in range(width_x):
+            value = start_ref[x, y]
+            pe[x + 2, y + 2] = value
+            a_send[0, x, y] = value.astype(jnp.bfloat16)
+        return carry
+
+    lax.fori_loop(0, width_y, keep_start, 0)
+    ge_recv[me] = geo_ref[...]
+    pl.semaphore_wait(barrier, count - 1)
+    others(count, me, lambda other: geo_copy(other, me).start())
+
+    last_layer = pl.ds(width_x - 1, 1)
+    per_iter = 12
+    for it in range(ITERS):
+        base_sem = it * per_iter
+        tr_send[it] = traces_of(
+            lambda x, y0: pe[x + 2, 2 + y0 : 2 + y0 + chunk]
+        )
+        tile = pl.multiple_of((v // group) * TILE, TILE)
+        tr_recv[it, v] = tr_send[it, pl.ds(tile, TILE), :]
+        others(vol_count, v, lambda other: trace_copy(it, other, v).start())
+        if it == 0:
+            near_mat = [
+                send_near(direction, mat_ref, mat_near.at[k], ITERS * per_iter + k)
+                for k, direction in enumerate(((1, 0), (-1, 0), (0, 1), (0, -1)))
+            ]
+        block = a_send.at[it]
+        got_x = [
+            send_near((1, 0), block.at[pl.ds(width_x - 2, 2)], ax.at[it, 0], base_sem),
+            send_near((-1, 0), block.at[pl.ds(0, 2)], ax.at[it, 1], base_sem + 1),
+        ]
+        got_y = [
+            send_near((0, 1), block.at[:, pl.ds(width_y - 2, 2)], ay.at[it, 0], base_sem + 2),
+            send_near((0, -1), block.at[:, pl.ds(0, 2)], ay.at[it, 1], base_sem + 3),
+        ]
+        got_c = []
+        for k, (dv, ds) in enumerate(((1, 1), (1, -1), (-1, 1), (-1, -1))):
+            x = width_x - 1 if dv > 0 else 0
+            y = width_y - 1 if ds > 0 else 0
+            got_c.append(
+                send_near((dv, ds), block.at[x, y], ac.at[it, k], base_sem + 4 + k)
+            )
+
+        others(vol_count, v, lambda other: trace_copy(it, other, other).wait_recv())
+        arrived = tr_recv[it].reshape(vol_count * TILE, LANES).T[:exc_count]
+        density = split_dot(arrived, merge_ref[...], NN).astype(jnp.bfloat16)
+        de_send[it] = density
+        de_recv[it, me] = density
+        others(count, me, lambda other: density_copy(it, other, me).start())
+
+        if it == 0:
+            others(count, me, lambda other: geo_copy(other, other).wait_recv())
+            lanes = lax.broadcasted_iota(jnp.int32, (TILE, LANES), 1)
+            mine = jnp.zeros((TILE, LANES), jnp.float32)
+            for w in range(vol_count):
+                piece = ge_recv[w * src_count]
+                for k in range(1, src_count):
+                    piece = piece + ge_recv[w * src_count + k]
+                ge_all[:, w * LANES : (w + 1) * LANES] = piece
+                shift = lax.rem(
+                    w * capacity + 2 * LANES - s * slot_count - v * capacity, LANES
+                )
+                turned = pltpu.roll(piece, shift, 1)
+                mine = mine + jnp.where(lanes // capacity == w, turned, 0.0)
+            columns = jnp.concatenate([mine] * (LANES // TILE), axis=0).T
+            columns = [columns[:, 3 + c : 4 + c] for c in range(3)]
+            for w in range(vol_count):
+                span = slice(w * LANES, (w + 1) * LANES)
+                slot_kernel[:, span] = pair_kernel(
+                    columns, [ge_all[c : c + 1, span] for c in range(3)]
+                )
+
+        others(count, me, lambda other: density_copy(it, other, other).wait_recv())
+        for w in range(vol_count):
+            piece = de_recv[it, w * src_count].astype(jnp.float32)
+            for k in range(1, src_count):
+                piece = piece + de_recv[it, w * src_count + k].astype(jnp.float32)
+            dens_all[:, w * LANES : (w + 1) * LANES] = piece.astype(jnp.bfloat16)
+        slot_flux = lax.dot_general(
+            dens_all[...], slot_kernel[...], NT, preferred_element_type=jnp.float32
+        )
+        back = slot_flux * flux_scale * slot_scale
+        for x in range(width_x):
+            for y0 in range(0, width_y, chunk):
+                spread = jnp.concatenate(
+                    [
+                        jnp.where(cell_row == x * width_y + y0 + k, back, 0.0)
+                        for k in range(chunk)
+                    ],
+                    axis=0,
+                )
+                surface = split_dot(spread, pick_depth, NT)
+                for k in range(chunk):
+                    forcing[x, y0 + k] = (
+                        exc_ref[x, y0 + k] + surface[k * exc_count : (k + 1) * exc_count]
+                    )
+
+        if it == 0:
+            for k, pair in enumerate(near_mat):
+                def zero(k=k):
+                    mat_near[k] = jnp.zeros(mat_ref.shape, jnp.int32)
+
+                land(pair[0], pair[1], lambda: None, zero)
+        rows, cols = pl.ds(2, width_x), pl.ds(2, width_y)
+        land_into(got_y[0], pe.at[rows, pl.ds(0, 2)], ay.at[it, 0])
+        land_into(got_y[1], pe.at[rows, pl.ds(width_y + 2, 2)], ay.at[it, 1])
+        for k, (dv, ds) in enumerate(((1, 1), (1, -1), (-1, 1), (-1, -1))):
+            x = 1 if dv > 0 else width_x + 2
+            y = 1 if ds > 0 else width_y + 2
+            land_into(got_c[k], pe.at[x, y], ac.at[it, k])
+        land_into(got_x[0], pe.at[pl.ds(0, 2), cols], ax.at[it, 0])
+        land_into(got_x[1], pe.at[pl.ds(width_x + 2, 2), cols], ax.at[it, 1])
+        all_nu()
+
+        def write_first(x, y, value):
+            pf[x + 1, y + 1] = value
+            b_send[it, x, y] = value.astype(jnp.bfloat16)
+
+        sweep(lambda x, y: pe[x + 2, y + 2], write_first)
+        block = b_send.at[it]
+        got_x = [
+            send_near((1, 0), block.at[last_layer], bx.at[it, 0], base_sem + 8),
+            send_near((-1, 0), block.at[pl.ds(0, 1)], bx.at[it, 1], base_sem + 9),
+        ]
+        got_y = [
+            send_near((0, 1), block.at[:, pl.ds(width_y - 1, 1)], by.at[it, 0], base_sem + 10),
+            send_near((0, -1), block.at[:, pl.ds(0, 1)], by.at[it, 1], base_sem + 11),
+        ]
+        if it == ITERS - 1:
+            target_block = 256
+
+            def one_block(index, carry):
+                span = pl.ds(pl.multiple_of(index * target_block, target_block), target_block)
+                points = target_ref[span, :]
+                columns = [points[:, c : c + 1] for c in range(3)]
+                total = jnp.zeros((target_block, exc_count), jnp.float32)
+                for k in range(0, vol_count * LANES, 2 * LANES):
+                    part = slice(k, k + 2 * LANES)
+                    tile = pair_kernel(columns, [ge_all[c : c + 1, part] for c in range(3)])
+                    total = total + lax.dot_general(
+                        tile, dens_all[:, part], NT, preferred_element_type=jnp.float32
+                    )
+                flux_ref[span, :] = total * flux_scale
+                return carry
+
+            lax.fori_loop(0, target_ref.shape[0] // target_block, one_block, 0)
+        rows, cols = pl.ds(1, width_x), pl.ds(1, width_y)
+        land_into(got_y[0], pf.at[rows, pl.ds(0, 1)], by.at[it, 0])
+        land_into(got_y[1], pf.at[rows, pl.ds(width_y + 1, 1)], by.at[it, 1])
+        land_into(got_x[0], pf.at[pl.ds(0, 1), cols], bx.at[it, 0])
+        land_into(got_x[1], pf.at[pl.ds(width_x + 1, 1), cols], bx.at[it, 1])
+
+        def write_second(x, y, value):
+            if it == ITERS - 1:
+                out_ref[x, y] = value
+            else:
+                pe[x + 2, y + 2] = value
+                a_send[it + 1, x, y] = value.astype(jnp.bfloat16)
+
+        sweep(lambda x, y: pf[x + 1, y + 1], write_second)
+
+    for sends, copy in started:
+        pl.when(sends)(copy.wait_send)
+    others(count, me, lambda other: geo_copy(other, me).wait_send())
+    for it in range(ITERS):
+        others(vol_count, v, lambda other: trace_copy(it, other, v).wait_send())
+        others(count, me, lambda other: density_copy(it, other, me).wait_send())
+
+
+def fused(
+    excitation, start, material, slot_cells, slot_scale, panels, target_points, source_points,
+):
+    vol_count, src_count = lax.axis_size("vol"), lax.axis_size("src")
+    v, s = lax.axis_index("vol"), lax.axis_index("src")
+    exc_count, width_x, width_y, depth = excitation.shape
+    slot_count = slot_cells.shape[0]
+    capacity = slot_count // vol_count
+    piece_len = source_points.shape[1] // vol_count
+    group = TILE // capacity
+    count = vol_count * src_count
+
+    def lane_rows(rows, fill):
+        rows = jnp.stack(rows)
+        return jnp.pad(
+            rows,
+            ((0, TILE - rows.shape[0]), (0, LANES - slot_count)),
+            constant_values=fill,
+        )
+
+    cells = lane_rows([slot_cells // depth, slot_cells % depth], -1)
+    scales = lane_rows([slot_scale], 0.0)
+    own_sources = lax.dynamic_slice_in_dim(source_points, v * piece_len, piece_len, 1)
+    own_targets = lax.dynamic_slice_in_dim(target_points, s * piece_len, piece_len, 1)
+    points = jnp.take(jnp.concatenate([own_sources, own_targets]), panels, axis=1)
+    points = jnp.pad(points, ((0, TILE - points.shape[0]), (0, 0)))
+    lane_live = jnp.arange(LANES) // slot_count == s
+    geometry = jnp.where(lane_live[None, :], jnp.tile(points, (1, src_count)), 0.0)
+    order = jnp.arange(slot_count)
+    earlier = (panels[:, None] == panels[None, :]) & (order[None, :] < order[:, None])
+    lane_panel = jnp.where(jnp.any(earlier, axis=1), -2, panels)
+    lane_panel = jnp.where(lane_live, jnp.tile(lane_panel, src_count), -2)
+    row_live = (jnp.arange(group) == v % group)[None, :, None]
+    row_panel = jnp.where(row_live, panels.reshape(vol_count, 1, capacity), -1).reshape(-1)
+    merge = (row_panel[:, None] == lane_panel[None, :]).astype(jnp.bfloat16)
+
+    vmem = pl.BlockSpec(memory_space=pltpu.VMEM)
+    field = (width_x, width_y, exc_count, depth)
+    plane = (exc_count, depth)
+    f32, bf16 = jnp.float32, jnp.bfloat16
+    halo_sems = ITERS * 12 + 4
+    sources = vol_count * LANES
+    dma = pltpu.SemaphoreType.DMA
+    potential, flux = pl.pallas_call(
+        functools.partial(
+            fused_kernel, vol_count, src_count, capacity, float(P_SIZE) ** (-0.5)
+        ),
+        out_shape=(
+            jax.ShapeDtypeStruct(field, f32),
+            jax.ShapeDtypeStruct((piece_len, exc_count), f32),
+        ),
+        in_specs=[vmem] * 8,
+        out_specs=(vmem, vmem),
+        scratch_shapes=[
+            pltpu.VMEM((width_x + 4, width_y + 4) + plane, f32),
+            pltpu.VMEM((width_x + 2, width_y + 2) + plane, f32),
+            pltpu.VMEM((width_x + 2, width_y + 2) + plane, f32),
+            pltpu.VMEM(field, f32),
+            pltpu.VMEM((ITERS,) + field, bf16),
+            pltpu.VMEM((ITERS, 2, 2, width_y) + plane, bf16),
+            pltpu.VMEM((ITERS, 2, width_x, 2) + plane, bf16),
+            pltpu.VMEM((ITERS, 4) + plane, bf16),
+            pltpu.VMEM((ITERS,) + field, bf16),
+            pltpu.VMEM((ITERS, 2, 1, width_y) + plane, bf16),
+            pltpu.VMEM((ITERS, 2, width_x, 1) + plane, bf16),
+            pltpu.VMEM((4, width_x, width_y, depth), jnp.int32),
+            pltpu.VMEM((ITERS, LANES, LANES), f32),
+            pltpu.VMEM((ITERS, vol_count, TILE, LANES), f32),
+            pltpu.VMEM((ITERS, exc_count, LANES), bf16),
+            pltpu.VMEM((ITERS, count, exc_count, LANES), bf16),
+            pltpu.VMEM((count, TILE, LANES), f32),
+            pltpu.VMEM((TILE, sources), f32),
+            pltpu.VMEM((LANES, sources), bf16),
+            pltpu.VMEM((exc_count, sources), bf16),
+            dma((halo_sems,)),
+            dma((halo_sems,)),
+            dma((ITERS, vol_count)),
+            dma((ITERS, vol_count)),
+            dma((ITERS, count)),
+            dma((ITERS, count)),
+            dma((count,)),
+            dma((count,)),
+        ],
+        compiler_params=pltpu.CompilerParams(
+            collective_id=0, has_side_effects=True, vmem_limit_bytes=40 * 1024 * 1024
+        ),
+    )(
+        start.transpose(1, 2, 0, 3),
+        excitation.transpose(1, 2, 0, 3),
+        material,
+        cells,
+        scales,
+        geometry,
+        merge,
+        own_targets.T,
+    )
+    return potential.transpose(2, 0, 1, 3), flux.T
 
 
 def per_device(
@@ -123,6 +615,22 @@
     slot_rank = jnp.arange(slot_count, dtype=jnp.int32) % capacity
     live_count = jnp.repeat(face_count.reshape(-1), capacity, total_repeat_length=slot_count)
     slot_scale = jnp.where(slot_rank < live_count, face_weight.reshape(-1), 0.0)
+    lane_tile = LANES == depth_len == slot_count * lax.axis_size("src")
+    if (
+        lane_tile
+        and vol_count * TILE == LANES
+        and TILE % capacity == 0
+        and LANES % exc_count == 0
+        and exc_count % 16 == 0
+        and width_x >= 2
+        and width_y % 8 == 0
+        and piece_len % 256 == 0
+        and piece_len * lax.axis_size("src") == target_len
+    ):
+        return fused(
+            excitation, start, material, slot_cells, slot_scale, slot_panel.reshape(-1),
+            target_points, source_points,
+        )
     compact = slot_count < piece_len
     vol_index = lax.axis_index("vol")
     src_index = lax.axis_index("src")

time: 259 us -> 91.2 us (0.35)
  blocking collectives: 85.4 us -> 0 us
  Pallas kernels: 0 us -> 76.7 us
  starting transfers between devices: 48.7 us -> 0 us
  waiting for transfers between devices: 47.3 us -> 0 us
  other arithmetic: 31 us -> 2.47 us
  local copies, waits for them, and re-layouts: 30.2 us -> 10.9 us
  matrix products: 12.4 us -> 0 us
    all_gather x2 -> x0, blocking collectives: 85.4 us -> none  [per_device(): gathered = lax.all_gather(message, ('vol', 'src'), axis=0, tiled=False)]
    pallas_call x0 -> x1, Pallas kernels: none -> 76.7 us  [fused(): pl.pallas_call(functools.partial(fused_kernel, vol_count, src_count, capa...]
    ppermute x24 -> x0, starting transfers between devices: 48.7 us -> none  [the longest x12 32.8 us: extended(): lax.ppermute(lax.slice_in_dim(block, block.shape[dim] - width, None, axis...]
    ppermute x24 -> x0, waiting for transfers between devices: 47.3 us -> none  [the longest x12 38.7 us: extended(): lax.ppermute(lax.slice_in_dim(block, block.shape[dim] - width, None, axis...]
    dot_general x5 -> x0, matrix products: 12.4 us -> none  [the longest x1 6.9 us: per_device(): jnp.einsum('ne,tn->et', density, kernel_block(own_targets, places), prefe...]
    add x6 -> x0, other arithmetic: 10.3 us -> none  [the longest x4 7.3 us: relax(): return center + RELAXATION * (forcing - applied) / diagonal]
    concatenate x9 -> x1, other arithmetic: 10.4 us -> 1.31 us  [fused(): jnp.concatenate([own_sources, own_targets])]
    slice x20 -> x0, local copies, waits for them, and re-layouts: 6.25 us -> none  [the longest x1 1.92 us: extended(): lax.slice_in_dim(block, 0, width, axis=dim)]
  transfers between devices with their start and end apart: 24 -> 0, of which waited for: 11 -> 0; matrix products, arithmetic and copies ran while one was open for 18% -> 0% of each run, Pallas kernels for 0% -> 0%
where the time goes in v2:
time: 91.2 us; the launch traced here: 90.9 us
  Pallas kernels  76.7 us (84%)
  local copies, waits for them, and re-layouts  10.9 us (12%)
  other arithmetic  2.47 us (3%)
    pallas_call x1, Pallas kernels, fused(): pl.pallas_call(functools.partial(fused_kernel, vol_count, src_count, capa...  76.7 us
    unnamed x24, local copies, waits for them, and re-layouts  5.99 us
    transpose x1, local copies, waits for them, and re-layouts, fused(): excitation.transpose(1, 2, 0, 3)  1.88 us

profile of v2, /device:TPU:0, one launch (start us, length us, event | category | flops | bytes accessed | tf_op | source)
XLA Modules:
  0.0 90.9 jit_solution(1088303752364388509)
XLA Ops:
  0.6 0.0 copy-start
  0.7 0.0 copy-start.6
  0.7 0.5 broadcast.320
  1.2 0.2 copy-done.6
  1.4 0.7 reduce.5
  2.0 0.2 fusion.1
  2.2 0.1 tile.21
  2.4 0.0 copy-start.7
  2.4 0.6 copy-done.7
  3.1 0.0 copy-start.5
  3.1 0.6 copy-done.5
  3.7 0.0 copy-start.2
  3.7 0.6 copy-done.2
  4.4 0.0 copy-start.8
  4.4 0.8 gather_fusion
  5.1 0.0 copy-done.8
  5.2 0.0 copy-start.4
  5.2 0.1 broadcast_in_dim.71
  5.3 0.1 broadcast_select_fusion
  5.3 0.1 select_n.146
  5.5 0.1 compare_convert_fusion.merge_ref
  5.6 0.4 copy-done.4
  6.0 0.0 copy-done
  6.0 0.4 copy.41
  6.4 0.4 copy.40
  6.8 0.0 copy-start.3
  6.8 1.3 %pad_maximum_fusion = f32[6,2048]{0,1:T(8,128)} fusion(f32[3,2048]{0,1:T(8,128)S(1)} %copy.41, f32[3,2048]{0,1:T(8,128)S(1)} %copy.40), kind=kLoop, calls=%fused_computation.2 | loop fusion | flops 12288 | bytes 98304 | tf_op jit(solution)/shard_map/concatenate | solution.py:516
  8.1 1.8 %gather_fusion.1 = f32[64,6]{1,0:T(8,128)S(1)} fusion(f32[6,2048]{0,1:T(8,128)} %pad_maximum_fusion, s32[1024]{0:T(1024)S(1)} %pad_clamp_fusion), kind=kCustom, calls=%fused_computation.1 | custom fusion | bytes 3328 | tf_op jit(solution)/shard_map/jit(_take)/gather | solution.py:516
  9.9 0.1 select_bitcast_fusion
  10.0 0.1 copy.42
  10.1 0.1 tile.9
  10.2 0.0 copy-done.3
  10.2 0.0 copy-start.1
  10.2 1.9 %copy_bitcast_fusion = (f32[2,16,32,128]{3,2,1,0:T(8,128)S(1)}, f32[2,16,32,128]{3,2,1,0:T(8,128)S(1)}) fusion(f32[32,2,16,128]{3,2,1,0:T(8,128)S(1)} %copy-done.3, f32[32,2,16,128]{3,2,1,0:T(8,128)} %param.12), kind=kLoop, calls=%fused_computation.3 | loop fusion | bytes 2097152 | tf_op jit(solution)/shard_map/transpose | solution.py:580
  12.1 0.0 copy-done.1
  12.1 76.7 %shard_map.104 = (f32[2,16,32,128]{3,2,1,0:T(8,128)S(1)}, f32[2048,32]{1,0:T(8,128)S(1)}) custom-call(f32[2,16,32,128]{3,2,1,0:T(8,128)S(1)} %get-tuple-element.29.start_ref, f32[2,16,32,128]{3,2,1,0:T(8,128)S(1)} %get-tuple-element.28.exc_ref, s32[2,16,128]{2,1,0:T(8,128)S(1)} %copy-done.1, s32[8,128]{1,0:T(8,128)S(1)} %pad.15.cell_ref, ...), custom_call_target="tpu_custom_call" | custom-call | tf_op jit(solution)/shard_map/pallas_call | solution.py:535
  88.8 1.1 %copy.38 = f32[32,2,16,128]{3,2,1,0:T(8,128)} copy(f32[32,2,16,128]{3,0,2,1:T(8,128)S(1)} %bitcast.38) | data formatting | bytes 1048576
  89.9 1.0 %copy.39 = f32[32,2048]{1,0:T(8,128)} copy(f32[32,2048]{0,1:T(8,128)S(1)} %bitcast.37) | data formatting | bytes 524288
  (19 shorter events, 0.1 us)
Async XLA Ops:
  0.6 5.4 %copy-start = (f32[3,32768]{1,0:T(4,128)S(1)}, f32[3,32768]{1,0:T(4,128)}, u32[]{:S(2)}) copy-start(f32[3,32768]{1,0:T(4,128)} %param.19) | copy-start | bytes 1179652
  0.7 0.7 copy-start.6
  2.4 0.7 copy-start.7
  3.1 0.7 copy-start.5
  3.7 0.7 copy-start.2
  4.4 0.8 copy-start.8
  5.2 0.8 copy-start.4
  6.8 3.4 %copy-start.3 = (f32[32,2,16,128]{3,2,1,0:T(8,128)S(1)}, f32[32,2,16,128]{3,2,1,0:T(8,128)}, u32[]{:S(2)}) copy-start(f32[32,2,16,128]{3,2,1,0:T(8,128)} %param.11) | copy-start | bytes 1572868
  10.2 1.9 %copy-start.1 = (s32[2,16,128]{2,1,0:T(8,128)S(1)}, s32[2,16,128]{2,1,0:T(8,128)}, u32[]{:S(2)}) copy-start(s32[2,16,128]{2,1,0:T(8,128)} %mat_ref.1) | copy-start | bytes 49156

commit v3 on v2

--- a/solution.py
+++ b/solution.py
@@ -117,6 +117,14 @@
     return total
 
 
+def one_hot(mask):
+    return jnp.where(mask, 1.0, 0.0).astype(jnp.bfloat16)
+
+
+def as_columns(rows):
+    return jnp.concatenate([rows] * (LANES // rows.shape[0]), axis=0).T
+
+
 def pair_kernel(columns, rows):
     dist_sq = None
     for column, row in zip(columns, rows):
@@ -127,11 +135,11 @@
 
 def fused_kernel(
     vol_count, src_count, capacity, flux_scale,
-    start_ref, exc_ref, mat_ref, cell_ref, scale_ref, geo_ref, merge_ref, target_ref,
+    start_ref, exc_ref, mat_ref, cell_ref, live_ref, weight_ref, panel_ref, target_ref, source_ref,
     out_ref, flux_ref,
     pe, pf, nu, forcing, a_send, ax, ay, ac, b_send, bx, by, mat_near,
     tr_send, tr_recv, de_send, de_recv, ge_recv, ge_all, slot_kernel, dens_all,
-    halo_ss, halo_rs, tr_ss, tr_rs, de_ss, de_rs, ge_ss, ge_rs,
+    points_ref, geo_ref, halo_ss, halo_rs, tr_ss, tr_rs, de_ss, de_rs, ge_ss, ge_rs,
 ):
     width_x, width_y, exc_count, depth = start_ref.shape
     count = vol_count * src_count
@@ -156,12 +164,28 @@
 
     lane = lax.broadcasted_iota(jnp.int32, (exc_count, depth), 1)
     at_low, at_high = lane == 0, lane == depth - 1
-    cell_row = cell_ref[0:1, :]
-    cell_depth = cell_ref[1:2, :]
-    slot_scale = scale_ref[0:1, :]
-    pick_depth = (
-        lax.broadcasted_iota(jnp.int32, (depth, LANES), 0) == cell_depth
-    ).astype(jnp.float32).astype(jnp.bfloat16)
+    row64 = lax.broadcasted_iota(jnp.int32, (slot_count, LANES), 0)
+    lane64 = lax.broadcasted_iota(jnp.int32, (slot_count, LANES), 1)
+    repeat_slots = one_hot(lane64 % slot_count == row64)
+
+    def spread_rows(ref, selector):
+        values = jnp.broadcast_to(ref[...].astype(jnp.float32), (TILE, ref.shape[1]))
+        return split_dot(values, selector, NN)
+
+    lane_row = lax.broadcasted_iota(jnp.int32, (1, LANES), 1)
+    lane_owner = lax.broadcasted_iota(jnp.int32, (vol_count, LANES), 1) % slot_count // capacity
+    pick_owner = one_hot(
+        lane_owner == lax.broadcasted_iota(jnp.int32, (vol_count, LANES), 0)
+    )
+    slot_cell = spread_rows(cell_ref, repeat_slots)[0:1].astype(jnp.int32)
+    slot_cell = jnp.where(lane_row < slot_count, slot_cell, -1)
+    cell_row = slot_cell >> (depth.bit_length() - 1)
+    cell_depth = jnp.where(slot_cell < 0, -1, slot_cell & (depth - 1))
+    live = (lane_row % capacity).astype(jnp.float32) < spread_rows(live_ref, pick_owner)[0:1]
+    slot_scale = jnp.where(
+        live & (lane_row < slot_count), spread_rows(weight_ref, repeat_slots)[0:1], 0.0
+    )
+    pick_depth = one_hot(lax.broadcasted_iota(jnp.int32, (depth, LANES), 0) == cell_depth)
     chunk = 8
 
     def traces_of(read):
@@ -176,7 +200,7 @@
                         cell_row == row, taken[k * exc_count : (k + 1) * exc_count], 0.0
                     )
         total = total * slot_scale
-        return jnp.concatenate([total] * (LANES // exc_count), axis=0).T
+        return as_columns(total)
 
     def each_near(direction):
         dv, ds = direction
@@ -250,6 +274,14 @@
 
         lax.fori_loop(1, total, step, 0)
 
+    def each_y(body):
+        def some(index, carry):
+            for k in range(4):
+                body(index * 4 + k)
+            return carry
+
+        lax.fori_loop(0, width_y // 4, some, 0)
+
     def depth_near(block, low_fill, high_fill):
         up = jnp.where(at_high, high_fill, pltpu.roll(block, depth - 1, 1))
         down = jnp.where(at_low, low_fill, pltpu.roll(block, 1, 1))
@@ -271,7 +303,7 @@
         return base + slope * grad_sq / (1.0 + grad_sq)
 
     def all_nu():
-        def one_y(y, carry):
+        def one_y(y):
             own = []
             for x in range(width_x):
                 value = nu_at(x, y, mat_ref[x, pl.ds(y, 1), :])
@@ -281,9 +313,8 @@
             high = nu_at(width_x, y, mat_near[1, 0, pl.ds(y, 1), :])
             nu[0, y + 1] = jnp.where(first_x, own[0], low)
             nu[width_x + 1, y + 1] = jnp.where(last_x, own[-1], high)
-            return carry
-
-        lax.fori_loop(0, width_y, one_y, 0)
+
+        each_y(one_y)
         for x in range(width_x):
             low = nu_at(x, -1, mat_near[2, x, width_y - 1 : width_y, :])
             high = nu_at(x, width_y, mat_near[3, x, 0:1, :])
@@ -312,24 +343,48 @@
         return center + RELAXATION * (forcing[x, y] - applied) / diagonal
 
     def sweep(read, write):
-        def one_y(y, carry):
+        def one_y(y):
             for x in range(width_x):
                 write(x, y, relaxed(read, x, y))
-            return carry
-
-        lax.fori_loop(0, width_y, one_y, 0)
-
-    def keep_start(y, carry):
+
+        each_y(one_y)
+
+    def keep_start(y):
         for x in range(width_x):
             value = start_ref[x, y]
             pe[x + 2, y + 2] = value
             a_send[0, x, y] = value.astype(jnp.bfloat16)
-        return carry
-
-    lax.fori_loop(0, width_y, keep_start, 0)
-    ge_recv[me] = geo_ref[...]
-    pl.semaphore_wait(barrier, count - 1)
-    others(count, me, lambda other: geo_copy(other, me).start())
+
+    each_y(keep_start)
+
+    def place_points():
+        piece_len = points_ref.shape[1]
+        points_ref[0:3, :] = source_ref[
+            :, pl.ds(pl.multiple_of(v * piece_len, LANES), piece_len)
+        ]
+        points_ref[3:6, :] = target_ref[
+            :, pl.ds(pl.multiple_of(s * piece_len, LANES), piece_len)
+        ]
+        points_ref[6:8, :] = jnp.zeros((2, piece_len), jnp.float32)
+        lane_panel = spread_rows(panel_ref, repeat_slots)
+        lane_index = lane_panel[0:1].astype(jnp.int32)
+        total = jnp.zeros((TILE, LANES), jnp.float32)
+        step = 256
+        for k in range(0, piece_len, step):
+            index = lax.broadcasted_iota(jnp.int32, (step, LANES), 0) + k
+            total = total + split_dot(
+                points_ref[:, k : k + step], one_hot(index == lane_index), NN
+            )
+        lane_live = lane_row // slot_count == s
+        geo_ref[...] = jnp.where(lane_live, total, 0.0)
+        row = lax.broadcasted_iota(jnp.int32, (LANES, LANES), 0)
+        column = lax.broadcasted_iota(jnp.int32, (LANES, LANES), 1)
+        earlier = (as_columns(lane_panel) == lane_panel[0:1]) & (row < column % slot_count)
+        repeated = jnp.sum(jnp.where(earlier, 1.0, 0.0), axis=0, keepdims=True)
+        arrival_slot = lane64 // TILE * capacity + lane64 % capacity
+        row_panel = as_columns(spread_rows(panel_ref, one_hot(arrival_slot == row64)))
+        keep = (row_panel == lane_panel[0:1]) & (repeated == 0.0) & lane_live
+        return one_hot(keep & (row % TILE // capacity == lax.rem(v, group)))
 
     last_layer = pl.ds(width_x - 1, 1)
     per_iter = 12
@@ -340,6 +395,8 @@
         )
         tile = pl.multiple_of((v // group) * TILE, TILE)
         tr_recv[it, v] = tr_send[it, pl.ds(tile, TILE), :]
+        if it == 0:
+            pl.semaphore_wait(barrier, count - 1)
         others(vol_count, v, lambda other: trace_copy(it, other, v).start())
         if it == 0:
             near_mat = [
@@ -363,9 +420,13 @@
                 send_near((dv, ds), block.at[x, y], ac.at[it, k], base_sem + 4 + k)
             )
 
+        if it == 0:
+            merge = place_points()
+            ge_recv[me] = geo_ref[...]
+            others(count, me, lambda other: geo_copy(other, me).start())
         others(vol_count, v, lambda other: trace_copy(it, other, other).wait_recv())
         arrived = tr_recv[it].reshape(vol_count * TILE, LANES).T[:exc_count]
-        density = split_dot(arrived, merge_ref[...], NN).astype(jnp.bfloat16)
+        density = split_dot(arrived, merge, NN).astype(jnp.bfloat16)
         de_send[it] = density
         de_recv[it, me] = density
         others(count, me, lambda other: density_copy(it, other, me).start())
@@ -384,7 +445,7 @@
                 )
                 turned = pltpu.roll(piece, shift, 1)
                 mine = mine + jnp.where(lanes // capacity == w, turned, 0.0)
-            columns = jnp.concatenate([mine] * (LANES // TILE), axis=0).T
+            columns = as_columns(mine)
             columns = [columns[:, 3 + c : 4 + c] for c in range(3)]
             for w in range(vol_count):
                 span = slice(w * LANES, (w + 1) * LANES)
@@ -453,8 +514,21 @@
 
             def one_block(index, carry):
                 span = pl.ds(pl.multiple_of(index * target_block, target_block), target_block)
-                points = target_ref[span, :]
-                columns = [points[:, c : c + 1] for c in range(3)]
+                points = jnp.concatenate(
+                    [
+                        as_columns(
+                            points_ref[
+                                :,
+                                pl.ds(
+                                    pl.multiple_of(index * target_block + k, LANES), LANES
+                                ),
+                            ]
+                        )
+                        for k in range(0, target_block, LANES)
+                    ],
+                    axis=0,
+                )
+                columns = [points[:, 3 + c : 4 + c] for c in range(3)]
                 total = jnp.zeros((target_block, exc_count), jnp.float32)
                 for k in range(0, vol_count * LANES, 2 * LANES):
                     part = slice(k, k + 2 * LANES)
@@ -465,7 +539,7 @@
                 flux_ref[span, :] = total * flux_scale
                 return carry
 
-            lax.fori_loop(0, target_ref.shape[0] // target_block, one_block, 0)
+            lax.fori_loop(0, points_ref.shape[1] // target_block, one_block, 0)
         rows, cols = pl.ds(1, width_x), pl.ds(1, width_y)
         land_into(got_y[0], pf.at[rows, pl.ds(0, 1)], by.at[it, 0])
         land_into(got_y[1], pf.at[rows, pl.ds(width_y + 1, 1)], by.at[it, 1])
@@ -490,41 +564,15 @@
 
 
 def fused(
-    excitation, start, material, slot_cells, slot_scale, panels, target_points, source_points,
+    excitation, start, material, face_cell, face_count, face_weight, slot_panel,
+    target_points, source_points,
 ):
     vol_count, src_count = lax.axis_size("vol"), lax.axis_size("src")
-    v, s = lax.axis_index("vol"), lax.axis_index("src")
     exc_count, width_x, width_y, depth = excitation.shape
-    slot_count = slot_cells.shape[0]
+    slot_count = face_cell.size
     capacity = slot_count // vol_count
     piece_len = source_points.shape[1] // vol_count
-    group = TILE // capacity
     count = vol_count * src_count
-
-    def lane_rows(rows, fill):
-        rows = jnp.stack(rows)
-        return jnp.pad(
-            rows,
-            ((0, TILE - rows.shape[0]), (0, LANES - slot_count)),
-            constant_values=fill,
-        )
-
-    cells = lane_rows([slot_cells // depth, slot_cells % depth], -1)
-    scales = lane_rows([slot_scale], 0.0)
-    own_sources = lax.dynamic_slice_in_dim(source_points, v * piece_len, piece_len, 1)
-    own_targets = lax.dynamic_slice_in_dim(target_points, s * piece_len, piece_len, 1)
-    points = jnp.take(jnp.concatenate([own_sources, own_targets]), panels, axis=1)
-    points = jnp.pad(points, ((0, TILE - points.shape[0]), (0, 0)))
-    lane_live = jnp.arange(LANES) // slot_count == s
-    geometry = jnp.where(lane_live[None, :], jnp.tile(points, (1, src_count)), 0.0)
-    order = jnp.arange(slot_count)
-    earlier = (panels[:, None] == panels[None, :]) & (order[None, :] < order[:, None])
-    lane_panel = jnp.where(jnp.any(earlier, axis=1), -2, panels)
-    lane_panel = jnp.where(lane_live, jnp.tile(lane_panel, src_count), -2)
-    row_live = (jnp.arange(group) == v % group)[None, :, None]
-    row_panel = jnp.where(row_live, panels.reshape(vol_count, 1, capacity), -1).reshape(-1)
-    merge = (row_panel[:, None] == lane_panel[None, :]).astype(jnp.bfloat16)
-
     vmem = pl.BlockSpec(memory_space=pltpu.VMEM)
     field = (width_x, width_y, exc_count, depth)
     plane = (exc_count, depth)
@@ -540,7 +588,7 @@
             jax.ShapeDtypeStruct(field, f32),
             jax.ShapeDtypeStruct((piece_len, exc_count), f32),
         ),
-        in_specs=[vmem] * 8,
+        in_specs=[vmem] * 9,
         out_specs=(vmem, vmem),
         scratch_shapes=[
             pltpu.VMEM((width_x + 4, width_y + 4) + plane, f32),
@@ -563,6 +611,8 @@
             pltpu.VMEM((TILE, sources), f32),
             pltpu.VMEM((LANES, sources), bf16),
             pltpu.VMEM((exc_count, sources), bf16),
+            pltpu.VMEM((TILE, piece_len), f32),
+            pltpu.VMEM((TILE, LANES), f32),
             dma((halo_sems,)),
             dma((halo_sems,)),
             dma((ITERS, vol_count)),
@@ -579,11 +629,12 @@
         start.transpose(1, 2, 0, 3),
         excitation.transpose(1, 2, 0, 3),
         material,
-        cells,
-        scales,
-        geometry,
-        merge,
-        own_targets.T,
+        face_cell.reshape(1, -1),
+        face_count.reshape(1, -1),
+        face_weight.reshape(1, -1),
+        slot_panel.reshape(1, -1),
+        target_points,
+        source_points,
     )
     return potential.transpose(2, 0, 1, 3), flux.T
 
@@ -612,9 +663,6 @@
     capacity = slot_count // vol_count
     piece_len = source_points.shape[1] // vol_count
     target_len = target_points.shape[1]
-    slot_rank = jnp.arange(slot_count, dtype=jnp.int32) % capacity
-    live_count = jnp.repeat(face_count.reshape(-1), capacity, total_repeat_length=slot_count)
-    slot_scale = jnp.where(slot_rank < live_count, face_weight.reshape(-1), 0.0)
     lane_tile = LANES == depth_len == slot_count * lax.axis_size("src")
     if (
         lane_tile
@@ -628,9 +676,12 @@
         and piece_len * lax.axis_size("src") == target_len
     ):
         return fused(
-            excitation, start, material, slot_cells, slot_scale, slot_panel.reshape(-1),
+            excitation, start, material, face_cell, face_count, face_weight, slot_panel,
             target_points, source_points,
         )
+    slot_rank = jnp.arange(slot_count, dtype=jnp.int32) % capacity
+    live_count = jnp.repeat(face_count.reshape(-1), capacity, total_repeat_length=slot_count)
+    slot_scale = jnp.where(slot_rank < live_count, face_weight.reshape(-1), 0.0)
     compact = slot_count < piece_len
     vol_index = lax.axis_index("vol")
     src_index = lax.axis_index("src")

time: 91.2 us -> 78 us (0.86)
  local copies, waits for them, and re-layouts: 10.9 us -> 4.62 us
  Pallas kernels: 76.7 us -> 72.5 us
  other arithmetic: 2.47 us -> 0 us
    pallas_call x1, Pallas kernels: 76.7 us -> 72.5 us  [fused(): pl.pallas_call(functools.partial(fused_kernel, vol_count, src_count, capa...]
    unnamed x24 -> x16, local copies, waits for them, and re-layouts: 5.99 us -> 2.76 us
    gather x2 -> x0, local copies, waits for them, and re-layouts: 2.6 us -> none  [the longest x1 1.82 us: fused(): jnp.take(jnp.concatenate([own_sources, own_targets]), panels, axis=1)]
    concatenate x1 -> x0, other arithmetic: 1.31 us -> none  [fused(): jnp.concatenate([own_sources, own_targets])]
where the time goes in v3:
time: 78 us; the launch traced here: 77.8 us
  Pallas kernels  72.5 us (93%)
  local copies, waits for them, and re-layouts  4.62 us (6%)
    pallas_call x1, Pallas kernels, fused(): pl.pallas_call(functools.partial(fused_kernel, vol_count, src_count, capa...  72.5 us
    unnamed x16, local copies, waits for them, and re-layouts  2.76 us
    transpose x1, local copies, waits for them, and re-layouts, fused(): excitation.transpose(1, 2, 0, 3)  1.87 us

profile of v3, /device:TPU:0, one launch (start us, length us, event | category | flops | bytes accessed | tf_op | source)
XLA Modules:
  0.0 77.8 jit_solution(2372158939339318940)
XLA Ops:
  0.6 0.0 copy-start
  0.6 0.0 copy-start.1
  0.7 0.0 copy-start.2
  0.7 0.0 copy-start.6
  0.7 1.9 %copy_bitcast_fusion = (f32[2,16,32,128]{3,2,1,0:T(8,128)S(1)}, f32[2,16,32,128]{3,2,1,0:T(8,128)S(1)}) fusion(f32[32,2,16,128]{3,2,1,0:T(8,128)} %param.9, f32[32,2,16,128]{3,2,1,0:T(8,128)} %param.10), kind=kLoop, calls=%fused_computation | loop fusion | bytes 2097152 | tf_op jit(solution)/shard_map/transpose | solution.py:630
  2.5 0.0 copy-start.3
  2.6 0.0 copy-start.4
  2.6 0.0 copy-start.5
  2.6 0.0 copy-done
  2.6 0.0 copy-done.1
  2.6 0.0 copy-done.2
  2.6 0.0 copy-done.6
  2.6 0.6 copy-done.3
  3.2 0.0 copy-done.4
  3.2 0.0 copy-done.5
  3.2 72.5 %shard_map.104 = (f32[2,16,32,128]{3,2,1,0:T(8,128)S(1)}, f32[2048,32]{1,0:T(8,128)S(1)}) custom-call(f32[2,16,32,128]{3,2,1,0:T(8,128)S(1)} %get-tuple-element.9.start_ref, f32[2,16,32,128]{3,2,1,0:T(8,128)S(1)} %get-tuple-element.8.exc_ref, s32[2,16,128]{2,1,0:T(8,128)S(1)} %copy-done.2, s32[1,64]{1,0:T(1,128)S(1)} %bitcast.12, s32[1,16]{1,0:T(1,128)S(1)} %bitcast.13, ...), custom_call_target="tpu_custom_call" | custom-call | tf_op jit(solution)/shard_map/pallas_call | solution.py:583
  75.7 1.1 %copy.13 = f32[32,2,16,128]{3,2,1,0:T(8,128)} copy(f32[32,2,16,128]{3,0,2,1:T(8,128)S(1)} %bitcast.11) | data formatting | bytes 1048576
  76.8 1.0 %copy.14 = f32[32,2048]{1,0:T(8,128)} copy(f32[32,2048]{0,1:T(8,128)S(1)} %bitcast.10) | data formatting | bytes 524288
Async XLA Ops:
  0.6 1.9 %copy-start = (f32[3,32768]{1,0:T(4,128)S(1)}, f32[3,32768]{1,0:T(4,128)}, u32[]{:S(2)}) copy-start(f32[3,32768]{1,0:T(4,128)} %source_ref.1) | copy-start | bytes 1179652
  0.6 1.9 %copy-start.1 = (f32[3,4096]{1,0:T(4,128)S(1)}, f32[3,4096]{1,0:T(4,128)}, u32[]{:S(2)}) copy-start(f32[3,4096]{1,0:T(4,128)} %target_ref.1) | copy-start | bytes 147460
  0.7 1.9 %copy-start.2 = (s32[2,16,128]{2,1,0:T(8,128)S(1)}, s32[2,16,128]{2,1,0:T(8,128)}, u32[]{:S(2)}) copy-start(s32[2,16,128]{2,1,0:T(8,128)} %mat_ref.1) | copy-start | bytes 49156
  0.7 1.9 %copy-start.6 = (s32[1,1,64]{2,1,0:T(1,128)S(1)}, s32[1,1,64]{2,1,0:T(1,128)}, u32[]{:S(2)}) copy-start(s32[1,1,64]{2,1,0:T(1,128)} %param.15) | copy-start | bytes 772
  2.5 0.7 copy-start.3
  2.6 0.7 copy-start.4
  2.6 0.7 copy-start.5

commit v4 on v3

--- a/solution.py
+++ b/solution.py
@@ -139,28 +139,36 @@
     out_ref, flux_ref,
     pe, pf, nu, forcing, a_send, ax, ay, ac, b_send, bx, by, mat_near,
     tr_send, tr_recv, de_send, de_recv, ge_recv, ge_all, slot_kernel, dens_all,
-    points_ref, geo_ref, halo_ss, halo_rs, tr_ss, tr_rs, de_ss, de_rs, ge_ss, ge_rs,
+    points_ref, geo_ref, ge_pair, ge_send, de_own, de_pair, gp_ss, gp_rs, dp_ss, dp_rs, halo_ss, halo_rs, tr_ss, tr_rs, de_ss, de_rs, ge_ss, ge_rs,
 ):
     width_x, width_y, exc_count, depth = start_ref.shape
-    count = vol_count * src_count
     v, s = lax.axis_index("vol"), lax.axis_index("src")
-    me = v * src_count + s
     group = TILE // capacity
     slot_count = vol_count * capacity
     first_x, last_x = v == 0, v == vol_count - 1
     first_y, last_y = s == 0, s == src_count - 1
 
-    def device(index):
-        return (index // src_count, lax.rem(index, src_count))
+    def others(total, own, body):
+        def step(index, carry):
+            body(lax.rem(own + index, total))
+            return carry
+
+        lax.fori_loop(1, total, step, 0)
 
     barrier = pltpu.get_barrier_semaphore()
 
-    def greet(step, carry):
-        other = lax.rem(me + step, count)
-        pl.semaphore_signal(barrier, inc=1, device_id=device(other), device_id_type=MESH)
-        return carry
-
-    lax.fori_loop(1, count, greet, 0)
+    def greet(v_other, s_other):
+        pl.semaphore_signal(
+            barrier, inc=1, device_id=(v_other, s_other), device_id_type=MESH
+        )
+
+    others(vol_count, v, lambda other: greet(other, s))
+    others(src_count, s, lambda other: greet(v, other))
+    near_x = jnp.where(first_x, 0, 1) + jnp.where(last_x, 0, 1)
+    near_y = jnp.where(first_y, 0, 1) + jnp.where(last_y, 0, 1)
+    for dv, in_x in ((1, jnp.logical_not(last_x)), (-1, jnp.logical_not(first_x))):
+        for ds, in_y in ((1, jnp.logical_not(last_y)), (-1, jnp.logical_not(first_y))):
+            pl.when(jnp.logical_and(in_x, in_y))(functools.partial(greet, v + dv, s + ds))
 
     lane = lax.broadcasted_iota(jnp.int32, (exc_count, depth), 1)
     at_low, at_high = lane == 0, lane == depth - 1
@@ -202,6 +210,12 @@
         total = total * slot_scale
         return as_columns(total)
 
+    def joined(pieces):
+        total = pieces[0]
+        for k in range(1, src_count):
+            total = total + pieces[k]
+        return total
+
     def each_near(direction):
         dv, ds = direction
         sends, gets = True, True
@@ -247,10 +261,24 @@
 
         land(pair[0], pair[1], put, zero)
 
+    def pair_copy(src, dst, send_sems, recv_sems, other, owner):
+        return pltpu.make_async_remote_copy(
+            src_ref=src, dst_ref=dst.at[owner], send_sem=send_sems.at[other],
+            recv_sem=recv_sems.at[owner], device_id=(v, other), device_id_type=MESH,
+        )
+
+    def geo_pair(other, owner):
+        return pair_copy(geo_ref, ge_pair, gp_ss, gp_rs, other, owner)
+
+    def density_pair(it, other, owner):
+        return pair_copy(
+            de_own.at[it], de_pair.at[it], dp_ss.at[it], dp_rs.at[it], other, owner
+        )
+
     def geo_copy(other, owner):
         return pltpu.make_async_remote_copy(
-            src_ref=geo_ref, dst_ref=ge_recv.at[owner], send_sem=ge_ss.at[other],
-            recv_sem=ge_rs.at[owner], device_id=device(other), device_id_type=MESH,
+            src_ref=ge_send, dst_ref=ge_recv.at[owner], send_sem=ge_ss.at[other],
+            recv_sem=ge_rs.at[owner], device_id=(other, s), device_id_type=MESH,
         )
 
     def trace_copy(it, other, owner):
@@ -264,15 +292,8 @@
     def density_copy(it, other, owner):
         return pltpu.make_async_remote_copy(
             src_ref=de_send.at[it], dst_ref=de_recv.at[it, owner], send_sem=de_ss.at[it, other],
-            recv_sem=de_rs.at[it, owner], device_id=device(other), device_id_type=MESH,
-        )
-
-    def others(total, own, body):
-        def step(index, carry):
-            body(lax.rem(own + index, total))
-            return carry
-
-        lax.fori_loop(1, total, step, 0)
+            recv_sem=de_rs.at[it, owner], device_id=(other, s), device_id_type=MESH,
+        )
 
     def each_y(body):
         def some(index, carry):
@@ -396,7 +417,7 @@
         tile = pl.multiple_of((v // group) * TILE, TILE)
         tr_recv[it, v] = tr_send[it, pl.ds(tile, TILE), :]
         if it == 0:
-            pl.semaphore_wait(barrier, count - 1)
+            pl.semaphore_wait(barrier, vol_count + src_count - 2 + near_x * near_y)
         others(vol_count, v, lambda other: trace_copy(it, other, v).start())
         if it == 0:
             near_mat = [
@@ -422,23 +443,30 @@
 
         if it == 0:
             merge = place_points()
-            ge_recv[me] = geo_ref[...]
-            others(count, me, lambda other: geo_copy(other, me).start())
+            ge_pair[s] = geo_ref[...]
+            others(src_count, s, lambda other: geo_pair(other, s).start())
+            others(src_count, s, lambda other: geo_pair(other, other).wait_recv())
+            ge_send[...] = joined(ge_pair[...])
+            ge_recv[v] = ge_send[...]
+            others(vol_count, v, lambda other: geo_copy(other, v).start())
         others(vol_count, v, lambda other: trace_copy(it, other, other).wait_recv())
         arrived = tr_recv[it].reshape(vol_count * TILE, LANES).T[:exc_count]
         density = split_dot(arrived, merge, NN).astype(jnp.bfloat16)
+        de_own[it] = density
+        de_pair[it, s] = density
+        others(src_count, s, lambda other: density_pair(it, other, s).start())
+        others(src_count, s, lambda other: density_pair(it, other, other).wait_recv())
+        density = joined(de_pair[it].astype(jnp.float32)).astype(jnp.bfloat16)
         de_send[it] = density
-        de_recv[it, me] = density
-        others(count, me, lambda other: density_copy(it, other, me).start())
+        de_recv[it, v] = density
+        others(vol_count, v, lambda other: density_copy(it, other, v).start())
 
         if it == 0:
-            others(count, me, lambda other: geo_copy(other, other).wait_recv())
+            others(vol_count, v, lambda other: geo_copy(other, other).wait_recv())
             lanes = lax.broadcasted_iota(jnp.int32, (TILE, LANES), 1)
             mine = jnp.zeros((TILE, LANES), jnp.float32)
             for w in range(vol_count):
-                piece = ge_recv[w * src_count]
-                for k in range(1, src_count):
-                    piece = piece + ge_recv[w * src_count + k]
+                piece = ge_recv[w]
                 ge_all[:, w * LANES : (w + 1) * LANES] = piece
                 shift = lax.rem(
                     w * capacity + 2 * LANES - s * slot_count - v * capacity, LANES
@@ -453,12 +481,9 @@
                     columns, [ge_all[c : c + 1, span] for c in range(3)]
                 )
 
-        others(count, me, lambda other: density_copy(it, other, other).wait_recv())
+        others(vol_count, v, lambda other: density_copy(it, other, other).wait_recv())
         for w in range(vol_count):
-            piece = de_recv[it, w * src_count].astype(jnp.float32)
-            for k in range(1, src_count):
-                piece = piece + de_recv[it, w * src_count + k].astype(jnp.float32)
-            dens_all[:, w * LANES : (w + 1) * LANES] = piece.astype(jnp.bfloat16)
+            dens_all[:, w * LANES : (w + 1) * LANES] = de_recv[it, w]
         slot_flux = lax.dot_general(
             dens_all[...], slot_kernel[...], NT, preferred_element_type=jnp.float32
         )
@@ -557,10 +582,12 @@
 
     for sends, copy in started:
         pl.when(sends)(copy.wait_send)
-    others(count, me, lambda other: geo_copy(other, me).wait_send())
+    others(src_count, s, lambda other: geo_pair(other, s).wait_send())
+    others(vol_count, v, lambda other: geo_copy(other, v).wait_send())
     for it in range(ITERS):
         others(vol_count, v, lambda other: trace_copy(it, other, v).wait_send())
-        others(count, me, lambda other: density_copy(it, other, me).wait_send())
+        others(src_count, s, lambda other: density_pair(it, other, s).wait_send())
+        others(vol_count, v, lambda other: density_copy(it, other, v).wait_send())
 
 
 def fused(
@@ -572,7 +599,6 @@
     slot_count = face_cell.size
     capacity = slot_count // vol_count
     piece_len = source_points.shape[1] // vol_count
-    count = vol_count * src_count
     vmem = pl.BlockSpec(memory_space=pltpu.VMEM)
     field = (width_x, width_y, exc_count, depth)
     plane = (exc_count, depth)
@@ -606,21 +632,29 @@
             pltpu.VMEM((ITERS, LANES, LANES), f32),
             pltpu.VMEM((ITERS, vol_count, TILE, LANES), f32),
             pltpu.VMEM((ITERS, exc_count, LANES), bf16),
-            pltpu.VMEM((ITERS, count, exc_count, LANES), bf16),
-            pltpu.VMEM((count, TILE, LANES), f32),
+            pltpu.VMEM((ITERS, vol_count, exc_count, LANES), bf16),
+            pltpu.VMEM((vol_count, TILE, LANES), f32),
             pltpu.VMEM((TILE, sources), f32),
             pltpu.VMEM((LANES, sources), bf16),
             pltpu.VMEM((exc_count, sources), bf16),
             pltpu.VMEM((TILE, piece_len), f32),
             pltpu.VMEM((TILE, LANES), f32),
+            pltpu.VMEM((src_count, TILE, LANES), f32),
+            pltpu.VMEM((TILE, LANES), f32),
+            pltpu.VMEM((ITERS, exc_count, LANES), bf16),
+            pltpu.VMEM((ITERS, src_count, exc_count, LANES), bf16),
+            dma((src_count,)),
+            dma((src_count,)),
+            dma((ITERS, src_count)),
+            dma((ITERS, src_count)),
             dma((halo_sems,)),
             dma((halo_sems,)),
             dma((ITERS, vol_count)),
             dma((ITERS, vol_count)),
-            dma((ITERS, count)),
-            dma((ITERS, count)),
-            dma((count,)),
-            dma((count,)),
+            dma((ITERS, vol_count)),
+            dma((ITERS, vol_count)),
+            dma((vol_count,)),
+            dma((vol_count,)),
         ],
         compiler_params=pltpu.CompilerParams(
             collective_id=0, has_side_effects=True, vmem_limit_bytes=40 * 1024 * 1024

time: 78 us -> 70.8 us (0.908)
  Pallas kernels: 72.5 us -> 65.3 us
    pallas_call x1, Pallas kernels: 72.5 us -> 65.3 us  [fused(): pl.pallas_call(functools.partial(fused_kernel, vol_count, src_count, capa...]
where the time goes in v4:
time: 70.8 us; the launch traced here: 70.6 us
  Pallas kernels  65.3 us (92%)
  local copies, waits for them, and re-layouts  4.62 us (7%)
  between operations  0.73 us (1%)
    pallas_call x1, Pallas kernels, fused(): pl.pallas_call(functools.partial(fused_kernel, vol_count, src_count, capa...  65.3 us
    unnamed x16, local copies, waits for them, and re-layouts  2.76 us
    transpose x1, local copies, waits for them, and re-layouts, fused(): excitation.transpose(1, 2, 0, 3)  1.87 us

profile of v4, /device:TPU:0, one launch (start us, length us, event | category | flops | bytes accessed | tf_op | source)
XLA Modules:
  0.0 70.6 jit_solution(11723750785047489251)
XLA Ops:
  0.6 0.0 copy-start
  0.6 0.0 copy-start.1
  0.7 0.0 copy-start.2
  0.7 0.0 copy-start.6
  0.7 1.9 %copy_bitcast_fusion = (f32[2,16,32,128]{3,2,1,0:T(8,128)S(1)}, f32[2,16,32,128]{3,2,1,0:T(8,128)S(1)}) fusion(f32[32,2,16,128]{3,2,1,0:T(8,128)} %param.9, f32[32,2,16,128]{3,2,1,0:T(8,128)} %param.10), kind=kLoop, calls=%fused_computation | loop fusion | bytes 2097152 | tf_op jit(solution)/shard_map/transpose | solution.py:664
  2.5 0.0 copy-start.3
  2.6 0.0 copy-start.4
  2.6 0.0 copy-start.5
  2.6 0.0 copy-done
  2.6 0.0 copy-done.1
  2.6 0.0 copy-done.2
  2.6 0.0 copy-done.6
  2.6 0.6 copy-done.3
  3.2 0.0 copy-done.4
  3.2 0.0 copy-done.5
  3.2 65.3 %shard_map.104 = (f32[2,16,32,128]{3,2,1,0:T(8,128)S(1)}, f32[2048,32]{1,0:T(8,128)S(1)}) custom-call(f32[2,16,32,128]{3,2,1,0:T(8,128)S(1)} %get-tuple-element.9.start_ref, f32[2,16,32,128]{3,2,1,0:T(8,128)S(1)} %get-tuple-element.8.exc_ref, s32[2,16,128]{2,1,0:T(8,128)S(1)} %copy-done.2, s32[1,64]{1,0:T(1,128)S(1)} %bitcast.12, s32[1,16]{1,0:T(1,128)S(1)} %bitcast.13, ...), custom_call_target="tpu_custom_call" | custom-call | tf_op jit(solution)/shard_map/pallas_call | solution.py:609
  68.5 1.1 %copy.13 = f32[32,2,16,128]{3,2,1,0:T(8,128)} copy(f32[32,2,16,128]{3,0,2,1:T(8,128)S(1)} %bitcast.11) | data formatting | bytes 1048576
  69.6 1.0 %copy.14 = f32[32,2048]{1,0:T(8,128)} copy(f32[32,2048]{0,1:T(8,128)S(1)} %bitcast.10) | data formatting | bytes 524288
Async XLA Ops:
  0.6 1.9 %copy-start = (f32[3,32768]{1,0:T(4,128)S(1)}, f32[3,32768]{1,0:T(4,128)}, u32[]{:S(2)}) copy-start(f32[3,32768]{1,0:T(4,128)} %source_ref.1) | copy-start | bytes 1179652
  0.6 1.9 %copy-start.1 = (f32[3,4096]{1,0:T(4,128)S(1)}, f32[3,4096]{1,0:T(4,128)}, u32[]{:S(2)}) copy-start(f32[3,4096]{1,0:T(4,128)} %target_ref.1) | copy-start | bytes 147460
  0.7 1.9 %copy-start.2 = (s32[2,16,128]{2,1,0:T(8,128)S(1)}, s32[2,16,128]{2,1,0:T(8,128)}, u32[]{:S(2)}) copy-start(s32[2,16,128]{2,1,0:T(8,128)} %mat_ref.1) | copy-start | bytes 49156
  0.7 1.9 %copy-start.6 = (s32[1,1,64]{2,1,0:T(1,128)S(1)}, s32[1,1,64]{2,1,0:T(1,128)}, u32[]{:S(2)}) copy-start(s32[1,1,64]{2,1,0:T(1,128)} %param.15) | copy-start | bytes 772
  2.5 0.7 copy-start.3
  2.6 0.7 copy-start.4
  2.6 0.7 copy-start.5

commit v5 on v4

--- a/solution.py
+++ b/solution.py
@@ -295,6 +295,13 @@
             recv_sem=de_rs.at[it, owner], device_id=(other, s), device_id_type=MESH,
         )
 
+    chunk_rows = 4
+    chunk_count = width_y // chunk_rows
+
+    def chunk_y(part, body):
+        for k in range(chunk_rows):
+            body(part * chunk_rows + k)
+
     def each_y(body):
         def some(index, carry):
             for k in range(4):
@@ -323,24 +330,26 @@
             slope = jnp.where(picked, NU_SATURATION[material_id], slope)
         return base + slope * grad_sq / (1.0 + grad_sq)
 
-    def all_nu():
+    def nu_chunk(part):
         def one_y(y):
             own = []
             for x in range(width_x):
-                value = nu_at(x, y, mat_ref[x, pl.ds(y, 1), :])
+                value = nu_at(x, y, mat_ref[x, y : y + 1, :])
                 nu[x + 1, y + 1] = value
                 own.append(value)
-            low = nu_at(-1, y, mat_near[0, width_x - 1, pl.ds(y, 1), :])
-            high = nu_at(width_x, y, mat_near[1, 0, pl.ds(y, 1), :])
+            low = nu_at(-1, y, mat_near[0, width_x - 1, y : y + 1, :])
+            high = nu_at(width_x, y, mat_near[1, 0, y : y + 1, :])
             nu[0, y + 1] = jnp.where(first_x, own[0], low)
             nu[width_x + 1, y + 1] = jnp.where(last_x, own[-1], high)
 
-        each_y(one_y)
+        chunk_y(part, one_y)
         for x in range(width_x):
-            low = nu_at(x, -1, mat_near[2, x, width_y - 1 : width_y, :])
-            high = nu_at(x, width_y, mat_near[3, x, 0:1, :])
-            nu[x + 1, 0] = jnp.where(first_y, nu[x + 1, 1], low)
-            nu[x + 1, width_y + 1] = jnp.where(last_y, nu[x + 1, width_y], high)
+            if part == 0:
+                low = nu_at(x, -1, mat_near[2, x, width_y - 1 : width_y, :])
+                nu[x + 1, 0] = jnp.where(first_y, nu[x + 1, 1], low)
+            if part == chunk_count - 1:
+                high = nu_at(x, width_y, mat_near[3, x, 0:1, :])
+                nu[x + 1, width_y + 1] = jnp.where(last_y, nu[x + 1, width_y], high)
 
     def relaxed(read, x, y):
         own = nu[x + 1, y + 1]
@@ -363,12 +372,12 @@
         applied = diagonal * center - pulled
         return center + RELAXATION * (forcing[x, y] - applied) / diagonal
 
-    def sweep(read, write):
+    def sweep(part, read, write):
         def one_y(y):
             for x in range(width_x):
                 write(x, y, relaxed(read, x, y))
 
-        each_y(one_y)
+        chunk_y(part, one_y)
 
     def keep_start(y):
         for x in range(width_x):
@@ -408,7 +417,7 @@
         return one_hot(keep & (row % TILE // capacity == lax.rem(v, group)))
 
     last_layer = pl.ds(width_x - 1, 1)
-    per_iter = 12
+    per_iter = 8 + width_y
     for it in range(ITERS):
         base_sem = it * per_iter
         tr_send[it] = traces_of(
@@ -425,20 +434,31 @@
                 for k, direction in enumerate(((1, 0), (-1, 0), (0, 1), (0, -1)))
             ]
         block = a_send.at[it]
-        got_x = [
-            send_near((1, 0), block.at[pl.ds(width_x - 2, 2)], ax.at[it, 0], base_sem),
-            send_near((-1, 0), block.at[pl.ds(0, 2)], ax.at[it, 1], base_sem + 1),
-        ]
+        got_x = []
+        for part in range(chunk_count):
+            span = pl.ds(part * chunk_rows, chunk_rows)
+            place = base_sem + 8 + 2 * part
+            got_x.append(
+                (
+                    send_near(
+                        (1, 0), block.at[pl.ds(width_x - 2, 2), span],
+                        ax.at[it, 0, :, span], place,
+                    ),
+                    send_near(
+                        (-1, 0), block.at[pl.ds(0, 2), span], ax.at[it, 1, :, span], place + 1
+                    ),
+                )
+            )
         got_y = [
-            send_near((0, 1), block.at[:, pl.ds(width_y - 2, 2)], ay.at[it, 0], base_sem + 2),
-            send_near((0, -1), block.at[:, pl.ds(0, 2)], ay.at[it, 1], base_sem + 3),
+            send_near((0, 1), block.at[:, pl.ds(width_y - 2, 2)], ay.at[it, 0], base_sem),
+            send_near((0, -1), block.at[:, pl.ds(0, 2)], ay.at[it, 1], base_sem + 1),
         ]
         got_c = []
         for k, (dv, ds) in enumerate(((1, 1), (1, -1), (-1, 1), (-1, -1))):
             x = width_x - 1 if dv > 0 else 0
             y = width_y - 1 if ds > 0 else 0
             got_c.append(
-                send_near((dv, ds), block.at[x, y], ac.at[it, k], base_sem + 4 + k)
+                send_near((dv, ds), block.at[x, y], ac.at[it, k], base_sem + 2 + k)
             )
 
         if it == 0:
@@ -509,30 +529,53 @@
                     mat_near[k] = jnp.zeros(mat_ref.shape, jnp.int32)
 
                 land(pair[0], pair[1], lambda: None, zero)
-        rows, cols = pl.ds(2, width_x), pl.ds(2, width_y)
+        rows = pl.ds(2, width_x)
         land_into(got_y[0], pe.at[rows, pl.ds(0, 2)], ay.at[it, 0])
         land_into(got_y[1], pe.at[rows, pl.ds(width_y + 2, 2)], ay.at[it, 1])
         for k, (dv, ds) in enumerate(((1, 1), (1, -1), (-1, 1), (-1, -1))):
             x = 1 if dv > 0 else width_x + 2
             y = 1 if ds > 0 else width_y + 2
             land_into(got_c[k], pe.at[x, y], ac.at[it, k])
-        land_into(got_x[0], pe.at[pl.ds(0, 2), cols], ax.at[it, 0])
-        land_into(got_x[1], pe.at[pl.ds(width_x + 2, 2), cols], ax.at[it, 1])
-        all_nu()
+
+        def land_outer(part):
+            span = pl.ds(part * chunk_rows, chunk_rows)
+            cols = pl.ds(2 + part * chunk_rows, chunk_rows)
+            low, high = got_x[part]
+            land_into(low, pe.at[pl.ds(0, 2), cols], ax.at[it, 0, :, span])
+            land_into(high, pe.at[pl.ds(width_x + 2, 2), cols], ax.at[it, 1, :, span])
 
         def write_first(x, y, value):
             pf[x + 1, y + 1] = value
             b_send[it, x, y] = value.astype(jnp.bfloat16)
 
-        sweep(lambda x, y: pe[x + 2, y + 2], write_first)
         block = b_send.at[it]
-        got_x = [
-            send_near((1, 0), block.at[last_layer], bx.at[it, 0], base_sem + 8),
-            send_near((-1, 0), block.at[pl.ds(0, 1)], bx.at[it, 1], base_sem + 9),
-        ]
+        got_b = []
+
+        def first_sweep(part):
+            sweep(part, lambda x, y: pe[x + 2, y + 2], write_first)
+            span = pl.ds(part * chunk_rows, chunk_rows)
+            place = base_sem + 8 + 2 * chunk_count + 2 * part
+            got_b.append(
+                (
+                    send_near((1, 0), block.at[last_layer, span], bx.at[it, 0, :, span], place),
+                    send_near(
+                        (-1, 0), block.at[pl.ds(0, 1), span], bx.at[it, 1, :, span], place + 1
+                    ),
+                )
+            )
+
+        for part in range(chunk_count + 2):
+            if part < chunk_count:
+                land_outer(part)
+            if 0 <= part - 1 < chunk_count:
+                nu_chunk(part - 1)
+            if 0 <= part - 2 < chunk_count:
+                first_sweep(part - 2)
         got_y = [
-            send_near((0, 1), block.at[:, pl.ds(width_y - 1, 1)], by.at[it, 0], base_sem + 10),
-            send_near((0, -1), block.at[:, pl.ds(0, 1)], by.at[it, 1], base_sem + 11),
+            send_near(
+                (0, 1), block.at[:, pl.ds(width_y - 1, 1)], by.at[it, 0], base_sem + 6
+            ),
+            send_near((0, -1), block.at[:, pl.ds(0, 1)], by.at[it, 1], base_sem + 7),
         ]
         if it == ITERS - 1:
             target_block = 256
@@ -565,12 +608,9 @@
                 return carry
 
             lax.fori_loop(0, points_ref.shape[1] // target_block, one_block, 0)
-        rows, cols = pl.ds(1, width_x), pl.ds(1, width_y)
+        rows = pl.ds(1, width_x)
         land_into(got_y[0], pf.at[rows, pl.ds(0, 1)], by.at[it, 0])
         land_into(got_y[1], pf.at[rows, pl.ds(width_y + 1, 1)], by.at[it, 1])
-        land_into(got_x[0], pf.at[pl.ds(0, 1), cols], bx.at[it, 0])
-        land_into(got_x[1], pf.at[pl.ds(width_x + 1, 1), cols], bx.at[it, 1])
-
         def write_second(x, y, value):
             if it == ITERS - 1:
                 out_ref[x, y] = value
@@ -578,7 +618,13 @@
                 pe[x + 2, y + 2] = value
                 a_send[it + 1, x, y] = value.astype(jnp.bfloat16)
 
-        sweep(lambda x, y: pf[x + 1, y + 1], write_second)
+        for part in range(chunk_count):
+            span = pl.ds(part * chunk_rows, chunk_rows)
+            cols = pl.ds(1 + part * chunk_rows, chunk_rows)
+            low, high = got_b[part]
+            land_into(low, pf.at[pl.ds(0, 1), cols], bx.at[it, 0, :, span])
+            land_into(high, pf.at[pl.ds(width_x + 1, 1), cols], bx.at[it, 1, :, span])
+            sweep(part, lambda x, y: pf[x + 1, y + 1], write_second)
 
     for sends, copy in started:
         pl.when(sends)(copy.wait_send)
@@ -603,7 +649,7 @@
     field = (width_x, width_y, exc_count, depth)
     plane = (exc_count, depth)
     f32, bf16 = jnp.float32, jnp.bfloat16
-    halo_sems = ITERS * 12 + 4
+    halo_sems = ITERS * (8 + width_y) + 4
     sources = vol_count * LANES
     dma = pltpu.SemaphoreType.DMA
     potential, flux = pl.pallas_call(

time: 70.8 us -> 68.8 us (0.972)
  Pallas kernels: 65.3 us -> 63.3 us
    pallas_call x1, Pallas kernels: 65.3 us -> 63.3 us  [fused(): pl.pallas_call(functools.partial(fused_kernel, vol_count, src_count, capa...]
where the time goes in v5:
time: 68.8 us; the launch traced here: 68.7 us
  Pallas kernels  63.3 us (92%)
  local copies, waits for them, and re-layouts  4.62 us (7%)
  between operations  0.73 us (1%)
    pallas_call x1, Pallas kernels, fused(): pl.pallas_call(functools.partial(fused_kernel, vol_count, src_count, capa...  63.3 us
    unnamed x16, local copies, waits for them, and re-layouts  2.76 us
    transpose x1, local copies, waits for them, and re-layouts, fused(): excitation.transpose(1, 2, 0, 3)  1.87 us

profile of v5, /device:TPU:0, one launch (start us, length us, event | category | flops | bytes accessed | tf_op | source)
XLA Modules:
  0.0 68.7 jit_solution(17266828845379762132)
XLA Ops:
  0.6 0.0 copy-start
  0.6 0.0 copy-start.1
  0.7 0.0 copy-start.2
  0.7 0.0 copy-start.6
  0.7 1.9 %copy_bitcast_fusion = (f32[2,16,32,128]{3,2,1,0:T(8,128)S(1)}, f32[2,16,32,128]{3,2,1,0:T(8,128)S(1)}) fusion(f32[32,2,16,128]{3,2,1,0:T(8,128)} %param.9, f32[32,2,16,128]{3,2,1,0:T(8,128)} %param.10), kind=kLoop, calls=%fused_computation | loop fusion | bytes 2097152 | tf_op jit(solution)/shard_map/transpose | solution.py:710
  2.5 0.0 copy-start.3
  2.6 0.0 copy-start.4
  2.6 0.0 copy-start.5
  2.6 0.0 copy-done
  2.6 0.0 copy-done.1
  2.6 0.0 copy-done.2
  2.6 0.0 copy-done.6
  2.6 0.6 copy-done.3
  3.2 0.0 copy-done.4
  3.2 0.0 copy-done.5
  3.2 63.3 %shard_map.104 = (f32[2,16,32,128]{3,2,1,0:T(8,128)S(1)}, f32[2048,32]{1,0:T(8,128)S(1)}) custom-call(f32[2,16,32,128]{3,2,1,0:T(8,128)S(1)} %get-tuple-element.9.start_ref, f32[2,16,32,128]{3,2,1,0:T(8,128)S(1)} %get-tuple-element.8.exc_ref, s32[2,16,128]{2,1,0:T(8,128)S(1)} %copy-done.2, s32[1,64]{1,0:T(1,128)S(1)} %bitcast.12, s32[1,16]{1,0:T(1,128)S(1)} %bitcast.13, ...), custom_call_target="tpu_custom_call" | custom-call | tf_op jit(solution)/shard_map/pallas_call | solution.py:655
  66.6 1.1 %copy.13 = f32[32,2,16,128]{3,2,1,0:T(8,128)} copy(f32[32,2,16,128]{3,0,2,1:T(8,128)S(1)} %bitcast.11) | data formatting | bytes 1048576
  67.7 1.0 %copy.14 = f32[32,2048]{1,0:T(8,128)} copy(f32[32,2048]{0,1:T(8,128)S(1)} %bitcast.10) | data formatting | bytes 524288
Async XLA Ops:
  0.6 1.9 %copy-start = (f32[3,32768]{1,0:T(4,128)S(1)}, f32[3,32768]{1,0:T(4,128)}, u32[]{:S(2)}) copy-start(f32[3,32768]{1,0:T(4,128)} %source_ref.1) | copy-start | bytes 1179652
  0.6 1.9 %copy-start.1 = (f32[3,4096]{1,0:T(4,128)S(1)}, f32[3,4096]{1,0:T(4,128)}, u32[]{:S(2)}) copy-start(f32[3,4096]{1,0:T(4,128)} %target_ref.1) | copy-start | bytes 147460
  0.7 1.9 %copy-start.2 = (s32[2,16,128]{2,1,0:T(8,128)S(1)}, s32[2,16,128]{2,1,0:T(8,128)}, u32[]{:S(2)}) copy-start(s32[2,16,128]{2,1,0:T(8,128)} %mat_ref.1) | copy-start | bytes 49156
  0.7 1.9 %copy-start.6 = (s32[1,1,64]{2,1,0:T(1,128)S(1)}, s32[1,1,64]{2,1,0:T(1,128)}, u32[]{:S(2)}) copy-start(s32[1,1,64]{2,1,0:T(1,128)} %param.15) | copy-start | bytes 772
  2.5 0.7 copy-start.3
  2.6 0.7 copy-start.4
  2.6 0.7 copy-start.5
